TPU v7x, 128 devices: a whole 4x4x4 slice. The times are simulated.
128 devices in a mesh: dp: 32 (over x, z, core), mp: 4 (over y).
Axes of the slice: x: 4, y: 4, z: 4, core: 2. Of those that a mesh axis runs over, the one named last changes fastest.
Arguments:
- embedding: bfloat16 [8192, 7168], P('dp', 'mp'), may hold values from -6 to 6
- hidden: bfloat16 [8192, 7168], P('dp', 'mp'), may hold values from -6 to 6
- embed_gain: float32 [7168], P('mp'), may hold values from 0.3 to 1.7
- hidden_gain: float32 [7168], P('mp'), may hold values from 0.3 to 1.7
- cotangent: bfloat16 [8192, 4096], P('dp', 'mp'), may hold values from -0.015625 to 0.015625
- left_stat: float32 [32768, 4096], P('dp', 'mp'), may hold values from -6 to 6
- right_stat: float32 [32768, 4096], P('dp', 'mp'), may hold values from -6 to 6
- left_root: bfloat16 [32768, 4096], P('dp', 'mp')
- right_root: bfloat16 [32768, 4096], P('dp', 'mp')
- owners: int32 [4, 14], replicated, may hold values from 0 to 31, as said below
Outputs:
- left_new: float32 [32768, 4096], P('dp', 'mp')
- right_new: float32 [32768, 4096], P('dp', 'mp')
- update: bfloat16 [4, 1024, 14336], P('mp', 'dp')
Inputs may be any that keep to these rules, and one draw needn't show every extreme that they name: In each block column the 14 owners are all different.
All inputs are finite; a program needn't handle non-finite values.
Results may differ from a plain program's by a relative error of at most 0.023.
Values may be sent and summed in bfloat16 or wider, within the bound.
A program may use at most 192 MiB of HBM per device.

v0:
```python
import jax
import jax.numpy as jnp
from jax import lax
from jax.sharding import PartitionSpec as P


def body(
    embedding,
    hidden,
    embed_gain,
    hidden_gain,
    cotangent,
    left_stat,
    right_stat,
    left_root,
    right_root,
    owners,
):
    stacked = jnp.stack([embedding, hidden], axis=1)
    values = stacked.astype(jnp.float32)
    squares = lax.psum(jnp.sum(values * values, axis=2), "mp")
    width = hidden.shape[1] * lax.axis_size("mp")
    scale = lax.rsqrt(squares / width + 1e-06)
    gains = jnp.stack([embed_gain, hidden_gain], axis=0)
    normed = (values * scale[:, :, None] * gains[None, :, :]).astype(jnp.bfloat16)
    total_in = 2 * width
    replicas = lax.axis_size("dp")
    side = cotangent.shape[1]
    sliver = side // replicas
    partial_value = jnp.einsum(
        "tb,thk->bhk",
        cotangent,
        lax.all_gather(normed, "mp", axis=2, tiled=True),
        preferred_element_type=jnp.float32,
    )
    share = lax.psum_scatter(
        partial_value.reshape(side, total_in).astype(jnp.bfloat16),
        "dp",
        scatter_dimension=0,
        tiled=True,
    ).astype(jnp.float32)
    share = share.astype(jnp.bfloat16)
    block_rows = total_in // side
    my_replica = lax.axis_index("dp")
    my_column = lax.axis_index("mp")
    column_owners = lax.dynamic_index_in_dim(owners, my_column, 0, keepdims=False)
    owner_hot = (column_owners[None, :] == jnp.arange(replicas, dtype=jnp.int32)[:, None]).astype(
        jnp.bfloat16
    )
    pieces = share.reshape(sliver, block_rows, side)
    outgoing = jnp.einsum(
        "or,srb->osb", owner_hot, pieces, preferred_element_type=jnp.float32
    ).astype(jnp.bfloat16)
    arrived = lax.all_to_all(outgoing, "dp", split_axis=0, concat_axis=1, tiled=True)
    grad_t = arrived.reshape(side, side)
    owned = jnp.any(column_owners == my_replica)
    gram_left = lax.dot_general(
        grad_t, grad_t, (((0,), (0,)), ((), ())), preferred_element_type=jnp.float32
    )
    gram_right = lax.dot_general(
        grad_t, grad_t, (((1,), (1,)), ((), ())), preferred_element_type=jnp.float32
    )
    left_new = jnp.where(owned, 0.9 * left_stat + 0.1 * gram_left, left_stat)
    right_new = jnp.where(owned, 0.9 * right_stat + 0.1 * gram_right, right_stat)
    inner_t = lax.dot_general(
        right_root, grad_t, (((0,), (0,)), ((), ())), preferred_element_type=jnp.float32
    ).astype(jnp.bfloat16)
    result_t = lax.dot_general(
        inner_t, left_root, (((1,), (1,)), ((), ())), preferred_element_type=jnp.float32
    ).astype(jnp.bfloat16)
    returned = lax.all_to_all(
        result_t.reshape(replicas, sliver, side), "dp", split_axis=0, concat_axis=0, tiled=True
    )
    placed = jnp.einsum(
        "or,osb->srb", owner_hot, returned, preferred_element_type=jnp.float32
    ).astype(jnp.bfloat16)
    update = placed.reshape(1, sliver, total_in)
    return (left_new, right_new, update)


def solution(mesh):
    placed = (
        P("dp", "mp"),
        P("dp", "mp"),
        P("mp"),
        P("mp"),
        P("dp", "mp"),
        P("dp", "mp"),
        P("dp", "mp"),
        P("dp", "mp"),
        P("dp", "mp"),
        P(),
    )
    return jax.shard_map(
        body,
        mesh=mesh,
        in_specs=placed,
        out_specs=(P("dp", "mp"), P("dp", "mp"), P("mp", "dp", None)),
        check_vma=False,
    )
```

profile of v0, /device:TPU:8, one launch (start us, length us, event | category | flops | bytes accessed | tf_op | source)
XLA Modules:
  0.0 398.7 jit_solution(72349972238462122)
XLA Ops:
  7.2 0.0 copy-start
  7.2 0.0 all-gather.2.cloned.1.call-start
  7.2 0.8 stack.22
  8.1 0.7 stack.21
  8.8 1.5 copy.27
  10.2 2.2 copy.26
  12.4 1.6 fusion.2
  14.0 8.7 %psum.7 = f32[256,2]{0,1:T(2,128)S(1)} all-reduce(f32[256,2]{0,1:T(2,128)S(1)} %fusion.2), channel_id=1, replica_groups=mesh['dp'=32,'mp'=4] {'mp'}, use_global_device_ids=true, to_apply=%region_2.0 | all-reduce | flops 512 | bytes 4096 | tf_op jit(solution)/shard_map/psum | solution.py:21
  22.8 0.0 copy-start.4
  22.8 2.6 fusion.4
  25.4 0.0 all-gather.2.cloned.1.call-update
  25.4 0.0 reduce-scatter.2.cloned.1.call-start
  25.5 76.3 %all-gather.2.cloned.1.call-done = bf16[256,2,7168]{0,2,1:T(8,128)(2,1)} async-done(((bf16[256,2,1792]{0,2,1:T(8,128)(2,1)}), bf16[256,2,7168]{0,2,1:T(8,128)(2,1)}) %all-gather.2.cloned.1.call-update) | async-done | bytes 7340048 | tf_op jit(solution)/shard_map/all_gather | solution.py:33
  101.8 0.0 copy-done.4
  101.8 15.7 %convolution_convert_fusion = bf16[2,7168,1024]{2,1,0:T(8,128)(2,1)} fusion(bf16[256,2,7168]{0,2,1:T(8,128)(2,1)} %all-gather.2.cloned.1.call-done, bf16[256,1024]{1,0:T(8,128)(2,1)S(1)} %copy-done.4), kind=kOutput, calls=%fused_computation | convolution fusion | flops 7530872832 | bytes 37224448 | tf_op jit(solution)/shard_map/tb,thk->bhk/dot_general | solution.py:30
  117.5 36.3 %copy.28 = bf16[1024,14336]{1,0:T(8,128)(2,1)} copy(bf16[1024,14336]{0,1:T(8,128)(2,1)} %bitcast.34) | data formatting | bytes 58720256 | tf_op jit(solution)/shard_map/convert_element_type | solution.py:37
  153.9 0.0 reduce-scatter.2.cloned.1.call-update
  153.9 1.3 compare_reduce_fusion
  155.2 153.5 %reduce-scatter.2.cloned.1.call-done = bf16[32,14336]{1,0:T(8,128)(2,1)} async-done(((bf16[1024,14336]{1,0:T(8,128)(2,1)}), bf16[32,14336]{1,0:T(8,128)(2,1)}) %reduce-scatter.2.cloned.1.call-update) | async-done | bytes 917520 | tf_op jit(solution)/shard_map/reduce_scatter | solution.py:36
  308.7 1.9 reshape.26
  310.6 0.8 convolution_convert_fusion.1
  311.4 1.2 copy.29
  312.6 32.7 %all_to_all.14 = bf16[32,32,1024]{2,1,0:T(8,128)(2,1)} all-to-all(bf16[32,32,1024]{2,1,0:T(8,128)(2,1)S(1)} %copy.29), channel_id=1, replica_groups=mesh['dp'=32,'mp'=4] {'dp'}, dimensions={0} | all-to-all | bytes 4194304 | tf_op jit(solution)/shard_map/all_to_all | solution.py:54
  345.3 8.1 %fusion.9 = bf16[1024,1024]{1,0:T(8,128)(2,1)} fusion(bf16[1024,1024]{1,0:T(8,128)(2,1)S(1)} %copy-done, bf16[1024,1024]{1,0:T(8,128)(2,1)} %bitcast.39, bf16[1024,1024]{1,0:T(8,128)(2,1)} %param.18), kind=kOutput, calls=%fused_computation.14 | convolution fusion | flops 4297064448 | bytes 8388608 | tf_op jit(solution)/shard_map/dot_general | solution.py:68
  353.4 5.1 %all-to-all-start.1 = ((bf16[32,32,1024]{2,1,0:T(8,128)(2,1)}), bf16[32,32,1024]{2,1,0:T(8,128)(2,1)}, u32[]{:S(2)}, u32[]{:S(2)}) async-start(bf16[32,32,1024]{2,1,0:T(8,128)(2,1)} %bitcast.41), calls=%async_computation.2 | async-start | bytes 4194304 | tf_op jit(solution)/shard_map/all_to_all | solution.py:71
  358.5 0.0 copy-start.5
  358.5 8.0 %add_select_fusion = f32[1024,1024]{1,0:T(8,128)} fusion(f32[1024,1024]{1,0:T(8,128)} %param.16, bf16[1024,1024]{1,0:T(8,128)(2,1)S(1)} %bitcast.40, pred[]{:T(512)} %get-tuple-element.3), kind=kOutput, calls=%fused_computation.6 | convolution fusion | flops 2151677952 | bytes 10485761 | tf_op jit(solution)/shard_map/dot_general | solution.py:60
  366.5 5.5 %fusion.1 = f32[1024,1024]{1,0:T(8,128)} fusion(f32[1024,1024]{1,0:T(8,128)S(1)} %copy-done.5, bf16[32,32,1024]{2,1,0:T(8,128)(2,1)S(1)} %copy-done.3, pred[]{:T(512)} %get-tuple-element.3), kind=kOutput, calls=%fused_computation.5 | convolution fusion | flops 2151677952 | bytes 10485761 | tf_op jit(solution)/shard_map/dot_general | solution.py:57
  372.0 15.3 %all-to-all-done.1 = bf16[32,32,1024]{2,1,0:T(8,128)(2,1)} async-done(((bf16[32,32,1024]{2,1,0:T(8,128)(2,1)}), bf16[32,32,1024]{2,1,0:T(8,128)(2,1)}, u32[]{:S(2)}, u32[]{:S(2)}) %all-to-all-start.1) | async-done | bytes 2097184 | tf_op jit(solution)/shard_map/all_to_all | solution.py:71
  387.3 2.9 fusion.15
  390.2 1.7 reshape.29
  391.9 0.0 copy-done.1
  (9 shorter events, 0.0 us)
Async XLA Ops:
  7.2 338.1 %copy-start = (bf16[1024,1024]{1,0:T(8,128)(2,1)S(1)}, bf16[1024,1024]{1,0:T(8,128)(2,1)}, u32[]{:S(2)}) copy-start(bf16[1024,1024]{1,0:T(8,128)(2,1)} %param.17) | copy-start | bytes 6291460
  7.2 94.7 %all-gather.2.cloned.1.call-start = ((), (), s32[]{:S(2)}) async-start(), calls=%async_computation.3 | async-start | bytes 9175040 | tf_op jit(solution)/shard_map/all_gather | solution.py:33
  22.8 79.1 %copy-start.4 = (bf16[256,1024]{1,0:T(8,128)(2,1)S(1)}, bf16[256,1024]{1,0:T(8,128)(2,1)}, u32[]{:S(2)}) copy-start(bf16[256,1024]{1,0:T(8,128)(2,1)} %param.14) | copy-start | bytes 1572868
  25.4 283.2 %reduce-scatter.2.cloned.1.call-start = ((), (), s32[]{:S(2)}) async-start(), calls=%async_computation.4 | async-start | bytes 30277632 | tf_op jit(solution)/shard_map/reduce_scatter | solution.py:36
  353.4 5.1 %copy-start.2 = (bf16[32,32,1024]{2,1,0:T(8,128)(2,1)S(1)}, bf16[32,32,1024]{2,1,0:T(8,128)(2,1)}, u32[]{:S(2)}) copy-start(bf16[32,32,1024]{2,1,0:T(8,128)(2,1)} %all_to_all.14) | copy-start | bytes 6291460
  353.4 34.0 %all-to-all-start.1 = ((bf16[32,32,1024]{2,1,0:T(8,128)(2,1)}), bf16[32,32,1024]{2,1,0:T(8,128)(2,1)}, u32[]{:S(2)}, u32[]{:S(2)}) async-start(bf16[32,32,1024]{2,1,0:T(8,128)(2,1)} %bitcast.41), calls=%async_computation.2 | async-start | bytes 4194304 | tf_op jit(solution)/shard_map/all_to_all | solution.py:71
  358.5 8.0 %copy-start.3 = (bf16[32,32,1024]{2,1,0:T(8,128)(2,1)S(1)}, bf16[32,32,1024]{2,1,0:T(8,128)(2,1)}, u32[]{:S(2)}) copy-start(bf16[32,32,1024]{2,1,0:T(8,128)(2,1)} %all_to_all.14) | copy-start | bytes 6291460
  358.5 8.0 %copy-start.5 = (f32[1024,1024]{1,0:T(8,128)S(1)}, f32[1024,1024]{1,0:T(8,128)}, u32[]{:S(2)}) copy-start(f32[1024,1024]{1,0:T(8,128)} %param.15) | copy-start | bytes 12582916
  366.5 25.4 %copy-start.1 = (bf16[1024,1024]{1,0:T(8,128)(2,1)S(1)}, bf16[1024,1024]{1,0:T(8,128)(2,1)}, u32[]{:S(2)}) copy-start(bf16[1024,1024]{1,0:T(8,128)(2,1)} %param.17) | copy-start | bytes 6291460
Sparse Core Ops, SparseCore 0:
  25.6 76.2 all-gather.1
  154.0 154.6 reduce-scatter.1
where the time goes:
time: 401 us; the launch traced here: 399 us
  waiting for transfers between devices  245 us (61%)
  local copies, waits for them, and re-layouts  46.4 us (12%)
  blocking collectives  41.4 us (10%)
  matrix products  40.9 us (10%)
  between operations  14.1 us (4%)
  other arithmetic  5.57 us (1%)
  starting transfers between devices  5.15 us (1%)
    reduce_scatter x1, waiting for transfers between devices, body(): lax.psum_scatter(partial_value.reshape(side, total_in).astype(jnp.bfloat1...  153 us
    all_gather x1, waiting for transfers between devices, body(): lax.all_gather(normed, 'mp', axis=2, tiled=True)  76.3 us
    convert_element_type x1, local copies, waits for them, and re-layouts, body(): partial_value.reshape(side, total_in).astype(jnp.bfloat16)  36.3 us
    all_to_all x1, blocking collectives, body(): lax.all_to_all(outgoing, 'dp', split_axis=0, concat_axis=1, tiled=True)  32.7 us
    dot_general x1, matrix products, body(): jnp.einsum('tb,thk->bhk', cotangent, lax.all_gather(normed, 'mp', axis=2,...  15.7 us
    all_to_all x1, waiting for transfers between devices, body(): lax.all_to_all(result_t.reshape(replicas, sliver, side), 'dp', split_axis...  15.3 us
    psum x1, blocking collectives, body(): squares = lax.psum(jnp.sum(values * values, axis=2), 'mp')  8.7 us
    dot_general x1, matrix products, body(): lax.dot_general(inner_t, left_root, (((1,), (1,)), ((), ())), preferred_e...  8.09 us
  transfers between devices with their start and end apart: 3, of which 3 were waited for; matrix products, arithmetic and copies ran while one was open for 4% of the time, Pallas kernels for 0%

commit v1 on v0

--- a/solution.py
+++ b/solution.py
@@ -1,7 +1,283 @@
+import functools
+
 import jax
 import jax.numpy as jnp
 from jax import lax
+from jax.experimental import pallas as pl
+from jax.experimental.pallas import tpu as pltpu
 from jax.sharding import PartitionSpec as P
+
+MESH = pl.DeviceIdType.MESH
+F32 = jnp.float32
+BF16 = jnp.bfloat16
+WIDTH = 7168
+PART = 1792
+HALF = 896
+DELTAS = (0, 1, 3, 2)
+
+
+def coords():
+    dp = lax.axis_index("dp")
+    return dp // 8, lax.axis_index("mp"), (dp // 2) % 4, dp % 2
+
+
+def device(x, y, z, core):
+    return ((x * 4 + z) * 2 + core, y)
+
+
+def remote(src, dst, send, recv, dest):
+    return pltpu.make_async_remote_copy(
+        src_ref=src, dst_ref=dst, send_sem=send, recv_sem=recv, device_id=dest, device_id_type=MESH
+    )
+
+
+def row_squares(ref):
+    acc = jnp.zeros((256, 128), F32)
+    for i in range(PART // 128):
+        v = ref[:, i * 128 : (i + 1) * 128].astype(F32)
+        acc = acc + v * v
+    return jnp.sum(jnp.transpose(acc), axis=0, keepdims=True)
+
+
+def reduce_kernel(
+    emb, hid, eg, hg, cot, share,
+    ct, nb, sq, sc, part, r1, q, r2, yb, sh,
+    sq_s, sq_r, sib_s, sib_r, ct_s, ct_r, rel_s, rel_r, p1_s, p1_r, p2_s, p2_r, y_s, y_r, loc,
+):
+    x, y, z, core = coords()
+    sib = device(x, y, z, 1 - core)
+    nbr = {
+        "x": (device((x + 1) % 4, y, z, core), device((x + 3) % 4, y, z, core), x),
+        "z": (device(x, y, (z + 1) % 4, core), device(x, y, (z + 3) % 4, core), z),
+    }
+    barrier = pltpu.get_barrier_semaphore()
+    peers = [sib]
+    for axis in ("x", "z"):
+        peers += [nbr[axis][0], nbr[axis][1]]
+    for d in (1, 2, 3):
+        peers += [device(x, (y + d) % 4, z, core), device(x, (y + d) % 4, z, 1 - core)]
+    for peer in peers:
+        pl.semaphore_signal(barrier, inc=1, device_id=peer, device_id_type=MESH)
+
+    ct[0, core] = jnp.transpose(cot[...]).reshape(4, 4, 64, 256)
+    sq[0] = jnp.concatenate([row_squares(emb), row_squares(hid), jnp.zeros((6, 256), F32)], axis=0)
+    pl.semaphore_wait(barrier, len(peers))
+
+    sends = []
+
+    def go(cp):
+        cp.start()
+        sends.append(cp)
+        return cp
+
+    sq_cp = [
+        go(remote(sq.at[0], sq.at[i], sq_s.at[i - 1], sq_r.at[i - 1], device(x, (y + i) % 4, z, core)))
+        for i in (1, 2, 3)
+    ]
+    ct_cp = {}
+    rel_cp = {}
+    rel_cp[0] = go(remote(ct.at[0, core], ct.at[0, core], rel_s.at[0], rel_r.at[0], sib))
+    for s in (1, 2, 3):
+        ct_cp[s] = go(
+            remote(ct.at[0, core], ct.at[s, core], ct_s.at[s - 1], ct_r.at[s - 1],
+                   device(x, (y + 4 - DELTAS[s]) % 4, z, core))
+        )
+    n_cp = remote(emb, nb.at[core], sib_s.at[0], sib_r.at[0], sib)
+    l_cp = pltpu.make_async_copy(emb, nb.at[core], loc.at[0])
+
+    @pl.when(core == 0)
+    def _():
+        remote(hid, nb.at[core], sib_s.at[0], sib_r.at[0], sib).start()
+        pltpu.make_async_copy(emb, nb.at[core], loc.at[0]).start()
+
+    @pl.when(core == 1)
+    def _():
+        remote(emb, nb.at[core], sib_s.at[0], sib_r.at[0], sib).start()
+        pltpu.make_async_copy(hid, nb.at[core], loc.at[0]).start()
+
+    sends.append(n_cp)
+    gain = jnp.where(core == 0, eg[...], hg[...])
+    for cp in sq_cp:
+        cp.wait_recv()
+    sc[core] = lax.rsqrt((sq[0] + sq[1] + sq[2] + sq[3]) / WIDTH + 1e-6)
+    sc_cp = go(remote(sc.at[core], sc.at[core], sib_s.at[1], sib_r.at[1], sib))
+    l_cp.wait()
+    n_cp.wait_recv()
+    sc_cp.wait_recv()
+    rel_cp[0].wait_recv()
+    scale = [jnp.where(core == 0, sc[t, 0:1], sc[t, 1:2]) for t in (0, 1)]
+
+    def relay(s):
+        ct_cp[s].wait_recv()
+        rel_cp[s] = go(remote(ct.at[s, core], ct.at[s, core], rel_s.at[s], rel_r.at[s], sib))
+
+    axes = (("x", "z"), ("z", "x"))
+    cps = {}
+
+    def product(s):
+        if s > 0:
+            rel_cp[s].wait_recv()
+
+        @pl.loop(0, 4)
+        def _(g):
+            xg = lax.rem(x + g, 4)
+            zg = lax.rem(z + g, 4)
+
+            def lhs(t, ab):
+                v = ct[s, t, xg] if ab == 0 else ct[s, t, :, zg]
+                return (v.reshape(256, 256).astype(F32) * scale[t]).astype(BF16)
+
+            for ab, at in ((0, xg), (1, zg)):
+                lanes = slice(ab * HALF, (ab + 1) * HALF)
+                acc = jnp.dot(lhs(0, ab), nb[0, :, lanes], preferred_element_type=F32)
+                acc = acc + jnp.dot(lhs(1, ab), nb[1, :, lanes], preferred_element_type=F32)
+                part[ab, s, at] = acc.astype(BF16).reshape(4, 64, HALF)
+
+    def ring1(ab, s):
+        plus, minus, pos = nbr[axes[ab][0]]
+        p1, m1, m2 = (pos + 1) % 4, (pos + 3) % 4, (pos + 2) % 4
+        src = part.at[ab, s]
+
+        def cp(i, ref, dest):
+            return remote(ref, r1.at[ab, s, i], p1_s.at[ab, s, i], p1_r.at[ab, s, i], dest)
+
+        return [
+            cp(0, src.at[m2, 0:2], plus),
+            cp(1, src.at[m2, 2:4], minus),
+            cp(2, src.at[p1, 2:4], plus),
+            cp(3, src.at[m1, 0:2], minus),
+            cp(4, src.at[p1, 0:2], plus),
+            cp(5, src.at[m1, 2:4], minus),
+        ], (pos, p1, m1)
+
+    def ring2(ab, s):
+        plus, minus, pos = nbr[axes[ab][1]]
+        p1, m1, m2 = (pos + 1) % 4, (pos + 3) % 4, (pos + 2) % 4
+        src = q.at[ab, s]
+
+        def cp(i, ref, dest):
+            return remote(ref, r2.at[ab, s, i], p2_s.at[ab, s, i], p2_r.at[ab, s, i], dest)
+
+        return [
+            cp(0, src.at[m2, 0:32], plus),
+            cp(1, src.at[m2, 32:64], minus),
+            cp(2, src.at[p1, 32:64], plus),
+            cp(3, src.at[m1, 0:32], minus),
+            cp(4, src.at[p1, 0:32], plus),
+            cp(5, src.at[m1, 32:64], minus),
+        ], (pos, p1, m1)
+
+    def add(a, *rest):
+        out = a.astype(F32)
+        for r in rest:
+            out = out + r.astype(F32)
+        return out
+
+    def stage_a(s):
+        product(s)
+        if s < 3:
+            relay(s + 1)
+        for ab in (0, 1):
+            cps[1, ab, s] = ring1(ab, s)
+            for i in range(4):
+                go(cps[1, ab, s][0][i])
+
+    def stage_b(s):
+        for ab in (0, 1):
+            c, (pos, p1, m1) = cps[1, ab, s]
+            c[0].wait_recv()
+            part[ab, s, p1, 0:2] = add(part[ab, s, p1, 0:2], r1[ab, s, 0]).astype(BF16)
+            go(c[4])
+            c[1].wait_recv()
+            part[ab, s, m1, 2:4] = add(part[ab, s, m1, 2:4], r1[ab, s, 1]).astype(BF16)
+            go(c[5])
+
+    def stage_c(s):
+        for ab in (0, 1):
+            c, (pos, p1, m1) = cps[1, ab, s]
+            for i in (2, 3, 4, 5):
+                c[i].wait_recv()
+            q[ab, s, 0:2] = add(part[ab, s, pos, 0:2], r1[ab, s, 4], r1[ab, s, 3]).astype(BF16)
+            q[ab, s, 2:4] = add(part[ab, s, pos, 2:4], r1[ab, s, 2], r1[ab, s, 5]).astype(BF16)
+            cps[2, ab, s] = ring2(ab, s)
+            for i in range(4):
+                go(cps[2, ab, s][0][i])
+
+    def stage_d(s):
+        for ab in (0, 1):
+            c, (pos, p1, m1) = cps[2, ab, s]
+            c[0].wait_recv()
+            q[ab, s, p1, 0:32] = add(q[ab, s, p1, 0:32], r2[ab, s, 0]).astype(BF16)
+            go(c[4])
+            c[1].wait_recv()
+            q[ab, s, m1, 32:64] = add(q[ab, s, m1, 32:64], r2[ab, s, 1]).astype(BF16)
+            go(c[5])
+
+    y_cp = []
+
+    def stage_e(s):
+        for ab in (0, 1):
+            c, (pos, p1, m1) = cps[2, ab, s]
+            for i in (2, 3, 4, 5):
+                c[i].wait_recv()
+            lanes = slice(ab * HALF, (ab + 1) * HALF)
+            g = gain[:, lanes]
+            yb[s, 0, :, lanes] = (add(q[ab, s, pos, 0:32], r2[ab, s, 4], r2[ab, s, 3]) * g).astype(BF16)
+            yb[s, 1, :, lanes] = (add(q[ab, s, pos, 32:64], r2[ab, s, 2], r2[ab, s, 5]) * g).astype(BF16)
+        for rel in (0, 1):
+            to = (core + rel) % 2
+            if s == 0 and rel == 0:
+                cp = pltpu.make_async_copy(yb.at[s, to], sh.at[core * 4 + y], loc.at[1])
+                cp.start()
+            else:
+                cp = go(
+                    remote(yb.at[s, to], sh.at[core * 4 + y], y_s.at[s, rel], y_r.at[s, rel],
+                           device(x, (y + DELTAS[s]) % 4, z, to))
+                )
+            y_cp.append(cp)
+
+    stages = {"a": stage_a, "b": stage_b, "c": stage_c, "d": stage_d, "e": stage_e}
+    for turn in range(8):
+        for behind, name in enumerate("abcde"):
+            if 0 <= turn - behind < 4:
+                stages[name](turn - behind)
+    for i, cp in enumerate(y_cp):
+        if i == 0:
+            cp.wait()
+        else:
+            cp.wait_recv()
+    for i in range(8):
+        share[:, i * PART : (i + 1) * PART] = sh[i]
+    for cp in sends:
+        cp.wait_send()
+
+
+def reduced_share(emb, hid, eg, hg, cot):
+    dma = pltpu.SemaphoreType.DMA
+    return pl.pallas_call(
+        reduce_kernel,
+        out_shape=jax.ShapeDtypeStruct((32, 2 * WIDTH), BF16),
+        in_specs=[pl.BlockSpec(memory_space=pltpu.VMEM)] * 5,
+        out_specs=pl.BlockSpec(memory_space=pltpu.VMEM),
+        scratch_shapes=[
+            pltpu.VMEM((4, 2, 4, 4, 64, 256), BF16),
+            pltpu.VMEM((2, 256, PART), BF16),
+            pltpu.VMEM((4, 8, 256), F32),
+            pltpu.VMEM((2, 8, 256), F32),
+            pltpu.VMEM((2, 4, 4, 4, 64, HALF), BF16),
+            pltpu.VMEM((2, 4, 6, 2, 64, HALF), BF16),
+            pltpu.VMEM((2, 4, 4, 64, HALF), BF16),
+            pltpu.VMEM((2, 4, 6, 32, HALF), BF16),
+            pltpu.VMEM((4, 2, 32, PART), BF16),
+            pltpu.VMEM((8, 32, PART), BF16),
+            dma((3,)), dma((3,)), dma((2,)), dma((2,)), dma((3,)), dma((3,)), dma((4,)), dma((4,)),
+            dma((2, 4, 6)), dma((2, 4, 6)), dma((2, 4, 6)), dma((2, 4, 6)), dma((4, 2)), dma((4, 2)), dma((2,)),
+        ],
+        compiler_params=pltpu.CompilerParams(
+            collective_id=0, has_side_effects=True, vmem_limit_bytes=60 * 2**20
+        ),
+        name="reduce_share",
+    )(emb, hid, eg, hg, cot)
 
 
 def body(
@@ -16,30 +292,11 @@
     right_root,
     owners,
 ):
-    stacked = jnp.stack([embedding, hidden], axis=1)
-    values = stacked.astype(jnp.float32)
-    squares = lax.psum(jnp.sum(values * values, axis=2), "mp")
-    width = hidden.shape[1] * lax.axis_size("mp")
-    scale = lax.rsqrt(squares / width + 1e-06)
-    gains = jnp.stack([embed_gain, hidden_gain], axis=0)
-    normed = (values * scale[:, :, None] * gains[None, :, :]).astype(jnp.bfloat16)
-    total_in = 2 * width
+    share = reduced_share(embedding, hidden, embed_gain[None], hidden_gain[None], cotangent)
+    total_in = share.shape[1]
     replicas = lax.axis_size("dp")
     side = cotangent.shape[1]
     sliver = side // replicas
-    partial_value = jnp.einsum(
-        "tb,thk->bhk",
-        cotangent,
-        lax.all_gather(normed, "mp", axis=2, tiled=True),
-        preferred_element_type=jnp.float32,
-    )
-    share = lax.psum_scatter(
-        partial_value.reshape(side, total_in).astype(jnp.bfloat16),
-        "dp",
-        scatter_dimension=0,
-        tiled=True,
-    ).astype(jnp.float32)
-    share = share.astype(jnp.bfloat16)
     block_rows = total_in // side
     my_replica = lax.axis_index("dp")
     my_column = lax.axis_index("mp")

time: 401 us -> 198 us (0.49)
  waiting for transfers between devices: 245 us -> 14.3 us
  Pallas kernels: 0 us -> 109 us
  local copies, waits for them, and re-layouts: 46.4 us -> 7.54 us
  matrix products: 40.9 us -> 26.4 us
  between operations: 14.1 us -> 0.7 us
  blocking collectives: 41.4 us -> 34 us
  other arithmetic: 5.57 us -> 1.33 us
    reduce_scatter x1 -> x0, waiting for transfers between devices: 153 us -> none  [body(): lax.psum_scatter(partial_value.reshape(side, total_in).astype(jnp.bfloat1...]
    pallas_call x0 -> x1, Pallas kernels: none -> 109 us  [reduced_share(): pl.pallas_call(reduce_kernel, out_shape=jax.ShapeDtypeStruct((32, 2 * WID...]
    all_gather x1 -> x0, waiting for transfers between devices: 76.3 us -> none  [body(): lax.all_gather(normed, 'mp', axis=2, tiled=True)]
    convert_element_type x1 -> x0, local copies, waits for them, and re-layouts: 36.3 us -> none  [body(): partial_value.reshape(side, total_in).astype(jnp.bfloat16)]
    dot_general x1 -> x0, matrix products: 15.7 us -> none  [body(): jnp.einsum('tb,thk->bhk', cotangent, lax.all_gather(normed, 'mp', axis=2,...]
    psum x1 -> x0, blocking collectives: 8.7 us -> none  [body(): squares = lax.psum(jnp.sum(values * values, axis=2), 'mp')]
  transfers between devices with their start and end apart: 3 -> 1, of which waited for: 3 -> 1; matrix products, arithmetic and copies ran while one was open for 4% -> 7% of each run, Pallas kernels for 0% -> 0%
where the time goes in v1:
time: 198 us
  Pallas kernels  109 us (55%)
  blocking collectives  34 us (17%)
  matrix products  26.4 us (13%)
  waiting for transfers between devices  14.3 us (7%)
  local copies, waits for them, and re-layouts  7.54 us (4%)
  starting transfers between devices  4.76 us (2%)
    pallas_call x1, Pallas kernels, reduced_share(): pl.pallas_call(reduce_kernel, out_shape=jax.ShapeDtypeStruct((32, 2 * WID...  109 us
    all_to_all x1, blocking collectives, body(): lax.all_to_all(outgoing, 'dp', split_axis=0, concat_axis=1, tiled=True)  34 us
    all_to_all x1, waiting for transfers between devices, body(): lax.all_to_all(result_t.reshape(replicas, sliver, side), 'dp', split_axis...  14.3 us
    dot_general x1, matrix products, body(): lax.dot_general(grad_t, grad_t, (((1,), (1,)), ((), ())), preferred_eleme...  9.25 us
    dot_general x1, matrix products, body(): lax.dot_general(inner_t, left_root, (((1,), (1,)), ((), ())), preferred_e...  8.09 us
    dot_general x1, matrix products, body(): lax.dot_general(grad_t, grad_t, (((0,), (0,)), ((), ())), preferred_eleme...  5.34 us
    all_to_all x1, starting transfers between devices, body(): lax.all_to_all(result_t.reshape(replicas, sliver, side), 'dp', split_axis...  4.76 us
  transfers between devices with their start and end apart: 1, of which 1 were waited for; matrix products, arithmetic and copies ran while one was open for 7% of the time, Pallas kernels for 0%

profile of v1, /device:TPU:8, one launch (start us, length us, event | category | flops | bytes accessed | tf_op | source)
XLA Modules:
  0.0 197.8 jit_solution(17975369008089281802)
XLA Ops:
  0.6 0.0 copy-start
  0.7 1.4 broadcast_in_dim.8.eg
  2.1 1.3 broadcast_in_dim.9.hg
  3.4 108.8 %reduce_share.1 = bf16[32,14336]{1,0:T(8,128)(2,1)} custom-call(bf16[256,1792]{1,0:T(8,128)(2,1)} %emb.1, bf16[256,1792]{1,0:T(8,128)(2,1)} %hid.1, f32[1,1792]{1,0:T(1,128)} %broadcast_in_dim.8.eg, f32[1,1792]{1,0:T(1,128)} %broadcast_in_dim.9.hg, bf16[256,1024]{1,0:T(8,128)(2,1)} %cot.1), custom_call_target="tpu_custom_call" | custom-call | tf_op jit(solution)/shard_map/reduce_share/pallas_call | solution.py:257
  112.2 1.9 reshape.22
  114.1 1.3 compare_reduce_fusion
  115.4 0.8 convolution_convert_fusion
  116.2 1.2 copy.20
  117.4 34.0 %all_to_all.14 = bf16[32,32,1024]{2,1,0:T(8,128)(2,1)} all-to-all(bf16[32,32,1024]{2,1,0:T(8,128)(2,1)S(1)} %copy.20), channel_id=1, replica_groups=mesh['dp'=32,'mp'=4] {'dp'}, dimensions={0} | all-to-all | bytes 4194304 | tf_op jit(solution)/shard_map/all_to_all | solution.py:311
  151.4 0.0 copy-done
  151.4 8.1 %fusion.6 = bf16[1024,1024]{1,0:T(8,128)(2,1)} fusion(bf16[1024,1024]{1,0:T(8,128)(2,1)S(1)} %copy-done, bf16[1024,1024]{1,0:T(8,128)(2,1)} %bitcast.25, bf16[1024,1024]{1,0:T(8,128)(2,1)} %param.18), kind=kOutput, calls=%fused_computation.8 | convolution fusion | flops 4297064448 | bytes 8388608 | tf_op jit(solution)/shard_map/dot_general | solution.py:325
  159.5 4.8 %all-to-all-start.1 = ((bf16[32,32,1024]{2,1,0:T(8,128)(2,1)}), bf16[32,32,1024]{2,1,0:T(8,128)(2,1)}, u32[]{:S(2)}, u32[]{:S(2)}) async-start(bf16[32,32,1024]{2,1,0:T(8,128)(2,1)} %bitcast.27), calls=%async_computation.1 | async-start | bytes 4194304 | tf_op jit(solution)/shard_map/all_to_all | solution.py:328
  164.3 0.0 copy-start.1
  164.3 0.0 copy-start.2
  164.3 9.3 %add_select_fusion = f32[1024,1024]{1,0:T(8,128)} fusion(f32[1024,1024]{1,0:T(8,128)} %param.16, bf16[1024,1024]{1,0:T(8,128)(2,1)} %bitcast.26, pred[]{:T(512)} %get-tuple-element.3), kind=kOutput, calls=%fused_computation.3 | convolution fusion | flops 2151677952 | bytes 10485761 | tf_op jit(solution)/shard_map/dot_general | solution.py:317
  173.6 0.0 copy-done.1
  173.6 0.0 copy-done.2
  173.6 5.3 %fusion.1 = f32[1024,1024]{1,0:T(8,128)} fusion(f32[1024,1024]{1,0:T(8,128)S(1)} %copy-done.2, bf16[32,32,1024]{2,1,0:T(8,128)(2,1)S(1)} %copy-done.1, pred[]{:T(512)} %get-tuple-element.3), kind=kOutput, calls=%fused_computation.2 | convolution fusion | flops 2151677952 | bytes 10485761 | tf_op jit(solution)/shard_map/dot_general | solution.py:314
  178.9 14.3 %all-to-all-done.1 = bf16[32,32,1024]{2,1,0:T(8,128)(2,1)} async-done(((bf16[32,32,1024]{2,1,0:T(8,128)(2,1)}), bf16[32,32,1024]{2,1,0:T(8,128)(2,1)}, u32[]{:S(2)}, u32[]{:S(2)}) %all-to-all-start.1) | async-done | bytes 2097184 | tf_op jit(solution)/shard_map/all_to_all | solution.py:328
  193.2 2.9 %fusion.12 = bf16[32,14,1024]{2,1,0:T(8,128)(2,1)S(1)} fusion(bf16[32,32,1024]{2,1,0:T(8,128)(2,1)} %all-to-all-done.1, s32[14]{0:T(128)S(1)} %get-tuple-element.4), kind=kOutput, calls=%fused_computation.11 | convolution fusion | flops 29819328 | bytes 3014712 | tf_op jit(solution)/shard_map/or,osb->srb/dot_general | solution.py:331
  196.0 1.7 reshape.25
Async XLA Ops:
  0.6 150.8 %copy-start = (bf16[1024,1024]{1,0:T(8,128)(2,1)S(1)}, bf16[1024,1024]{1,0:T(8,128)(2,1)}, u32[]{:S(2)}) copy-start(bf16[1024,1024]{1,0:T(8,128)(2,1)} %param.17) | copy-start | bytes 6291460
  159.5 33.6 %all-to-all-start.1 = ((bf16[32,32,1024]{2,1,0:T(8,128)(2,1)}), bf16[32,32,1024]{2,1,0:T(8,128)(2,1)}, u32[]{:S(2)}, u32[]{:S(2)}) async-start(bf16[32,32,1024]{2,1,0:T(8,128)(2,1)} %bitcast.27), calls=%async_computation.1 | async-start | bytes 4194304 | tf_op jit(solution)/shard_map/all_to_all | solution.py:328
  164.3 9.3 %copy-start.1 = (bf16[32,32,1024]{2,1,0:T(8,128)(2,1)S(1)}, bf16[32,32,1024]{2,1,0:T(8,128)(2,1)}, u32[]{:S(2)}) copy-start(bf16[32,32,1024]{2,1,0:T(8,128)(2,1)} %all_to_all.14) | copy-start | bytes 6291460
  164.3 9.3 %copy-start.2 = (f32[1024,1024]{1,0:T(8,128)S(1)}, f32[1024,1024]{1,0:T(8,128)}, u32[]{:S(2)}) copy-start(f32[1024,1024]{1,0:T(8,128)} %param.15) | copy-start | bytes 12582916

commit v2 on v1

--- a/solution.py
+++ b/solution.py
@@ -40,9 +40,10 @@
 
 
 def reduce_kernel(
-    emb, hid, eg, hg, cot, share,
-    ct, nb, sq, sc, part, r1, q, r2, yb, sh,
+    emb, hid, eg, hg, cot, own, lstat, rstat, lroot, rroot, lnew, rnew, update,
+    ct, nb, sq, sc, part, r1, r2, yb, sh, blocks, outb, arr, ret, tb, rt, lt, st, so,
     sq_s, sq_r, sib_s, sib_r, ct_s, ct_r, rel_s, rel_r, p1_s, p1_r, p2_s, p2_r, y_s, y_r, loc,
+    o_s, o_r, b_s, b_r, st_i, st_o,
 ):
     x, y, z, core = coords()
     sib = device(x, y, z, 1 - core)
@@ -51,17 +52,26 @@
         "z": (device(x, y, (z + 1) % 4, core), device(x, y, (z + 3) % 4, core), z),
     }
     barrier = pltpu.get_barrier_semaphore()
-    peers = [sib]
-    for axis in ("x", "z"):
-        peers += [nbr[axis][0], nbr[axis][1]]
+    me = (x * 4 + z) * 2 + core
+
+    def peer_of(k):
+        tx, tz, tc = (x + k // 8) % 4, (z + (k // 2) % 4) % 4, (core + k % 2) % 2
+        return (tx * 4 + tz) * 2 + tc
+
     for d in (1, 2, 3):
-        peers += [device(x, (y + d) % 4, z, core), device(x, (y + d) % 4, z, 1 - core)]
-    for peer in peers:
-        pl.semaphore_signal(barrier, inc=1, device_id=peer, device_id_type=MESH)
+        for c in (core, 1 - core):
+            pl.semaphore_signal(barrier, inc=1, device_id=device(x, (y + d) % 4, z, c), device_id_type=MESH)
+
+    @pl.loop(1, 32)
+    def _(k):
+        pl.semaphore_signal(barrier, inc=1, device_id=(peer_of(k), y), device_id_type=MESH)
+
+    r_cp = pltpu.make_async_copy(rroot, tb, loc.at[2])
+    r_cp.start()
 
     ct[0, core] = jnp.transpose(cot[...]).reshape(4, 4, 64, 256)
     sq[0] = jnp.concatenate([row_squares(emb), row_squares(hid), jnp.zeros((6, 256), F32)], axis=0)
-    pl.semaphore_wait(barrier, len(peers))
+    pl.semaphore_wait(barrier, 37)
 
     sends = []
 
@@ -153,7 +163,7 @@
     def ring2(ab, s):
         plus, minus, pos = nbr[axes[ab][1]]
         p1, m1, m2 = (pos + 1) % 4, (pos + 3) % 4, (pos + 2) % 4
-        src = q.at[ab, s]
+        src = part.at[ab, s, nbr[axes[ab][0]][2]]
 
         def cp(i, ref, dest):
             return remote(ref, r2.at[ab, s, i], p2_s.at[ab, s, i], p2_r.at[ab, s, i], dest)
@@ -197,8 +207,8 @@
             c, (pos, p1, m1) = cps[1, ab, s]
             for i in (2, 3, 4, 5):
                 c[i].wait_recv()
-            q[ab, s, 0:2] = add(part[ab, s, pos, 0:2], r1[ab, s, 4], r1[ab, s, 3]).astype(BF16)
-            q[ab, s, 2:4] = add(part[ab, s, pos, 2:4], r1[ab, s, 2], r1[ab, s, 5]).astype(BF16)
+            part[ab, s, pos, 0:2] = add(part[ab, s, pos, 0:2], r1[ab, s, 4], r1[ab, s, 3]).astype(BF16)
+            part[ab, s, pos, 2:4] = add(part[ab, s, pos, 2:4], r1[ab, s, 2], r1[ab, s, 5]).astype(BF16)
             cps[2, ab, s] = ring2(ab, s)
             for i in range(4):
                 go(cps[2, ab, s][0][i])
@@ -207,10 +217,11 @@
         for ab in (0, 1):
             c, (pos, p1, m1) = cps[2, ab, s]
             c[0].wait_recv()
-            q[ab, s, p1, 0:32] = add(q[ab, s, p1, 0:32], r2[ab, s, 0]).astype(BF16)
+            o = nbr[axes[ab][0]][2]
+            part[ab, s, o, p1, 0:32] = add(part[ab, s, o, p1, 0:32], r2[ab, s, 0]).astype(BF16)
             go(c[4])
             c[1].wait_recv()
-            q[ab, s, m1, 32:64] = add(q[ab, s, m1, 32:64], r2[ab, s, 1]).astype(BF16)
+            part[ab, s, o, m1, 32:64] = add(part[ab, s, o, m1, 32:64], r2[ab, s, 1]).astype(BF16)
             go(c[5])
 
     y_cp = []
@@ -222,8 +233,9 @@
                 c[i].wait_recv()
             lanes = slice(ab * HALF, (ab + 1) * HALF)
             g = gain[:, lanes]
-            yb[s, 0, :, lanes] = (add(q[ab, s, pos, 0:32], r2[ab, s, 4], r2[ab, s, 3]) * g).astype(BF16)
-            yb[s, 1, :, lanes] = (add(q[ab, s, pos, 32:64], r2[ab, s, 2], r2[ab, s, 5]) * g).astype(BF16)
+            o = nbr[axes[ab][0]][2]
+            yb[s, 0, :, lanes] = (add(part[ab, s, o, pos, 0:32], r2[ab, s, 4], r2[ab, s, 3]) * g).astype(BF16)
+            yb[s, 1, :, lanes] = (add(part[ab, s, o, pos, 32:64], r2[ab, s, 2], r2[ab, s, 5]) * g).astype(BF16)
         for rel in (0, 1):
             to = (core + rel) % 2
             if s == 0 and rel == 0:
@@ -237,28 +249,153 @@
             y_cp.append(cp)
 
     stages = {"a": stage_a, "b": stage_b, "c": stage_c, "d": stage_d, "e": stage_e}
+    def transpose_root(out):
+        @pl.loop(0, 8)
+        def _(i):
+            at = pl.ds(pl.multiple_of(i * 128, 128), 128)
+            out[at, :] = jnp.transpose(tb[:, at])
+
+    def stat_in(i, side):
+        rows = pl.ds(pl.multiple_of(i * 256, 256), 256)
+        return pltpu.make_async_copy((lstat, rstat)[side].at[rows], st.at[side], st_i.at[side])
+
+    def stat_out(i, side):
+        rows = pl.ds(pl.multiple_of(i * 256, 256), 256)
+        return pltpu.make_async_copy(so.at[side], (lnew, rnew)[side].at[rows], st_o.at[side])
+
     for turn in range(8):
         for behind, name in enumerate("abcde"):
             if 0 <= turn - behind < 4:
                 stages[name](turn - behind)
+        if turn == 3:
+            r_cp.wait()
+            transpose_root(rt)
+            l_root = pltpu.make_async_copy(lroot, tb, loc.at[3])
+            l_root.start()
+        if turn == 4:
+            l_root.wait()
+            transpose_root(lt)
+            stat_in(0, 0).start()
+            stat_in(0, 1).start()
     for i, cp in enumerate(y_cp):
         if i == 0:
             cp.wait()
         else:
             cp.wait_recv()
-    for i in range(8):
-        share[:, i * PART : (i + 1) * PART] = sh[i]
+
+    for r in range(14):
+        at = r * 1024
+        done = 0
+        while done < 1024:
+            i, lane = (at + done) // PART, (at + done) % PART
+            size = min(1024 - done, PART - lane)
+            blocks[r, :, done : done + size] = sh[i, :, lane : lane + size]
+            done += size
+
+    owner_of = [own[y, r] for r in range(14)]
+
+    def row_of(d):
+        row = jnp.int32(0)
+        for r in range(14):
+            row = jnp.where(owner_of[r] == d, jnp.int32(r), row)
+        return row
+
+    def to_owner(k):
+        t = peer_of(k)
+        return t, remote(outb.at[t], arr.at[me], o_s.at[k], o_r.at[k], (t, y))
+
+    def back(k):
+        t = peer_of(k)
+        return t, remote(outb.at[t], ret.at[me], b_s.at[k], b_r.at[k], (t, y))
+
+    @pl.loop(1, 32)
+    def _(k):
+        t, cp = to_owner(k)
+        outb[t] = blocks[row_of(t)]
+        cp.start()
+
+    arr[me] = blocks[row_of(me)]
+    mine = jnp.int32(0)
+    for r in range(14):
+        mine = jnp.where(owner_of[r] == me, jnp.int32(1), mine)
     for cp in sends:
         cp.wait_send()
 
-
-def reduced_share(emb, hid, eg, hg, cot):
+    @pl.loop(1, 32)
+    def _(k):
+        _, cp = to_owner(k)
+        cp.wait()
+
+    @pl.loop(0, 4)
+    def _(i):
+        g = lax.rem(i + 1, 4)
+        tx = lax.rem(x + g, 4)
+        rows = pl.ds(pl.multiple_of(tx * 256, 256), 256)
+        inner = jnp.dot(
+            rt[rows, :], arr[...].reshape(1024, 1024), preferred_element_type=F32
+        ).astype(BF16)
+        res = jnp.dot(inner, lt[...], preferred_element_type=F32).astype(BF16)
+        outb[pl.ds(tx * 8, 8)] = res.reshape(8, 32, 1024)
+        for j in range(8):
+            k = g * 8 + j
+
+            @pl.when(k > 0)
+            def _():
+                back(k)[1].start()
+
+    ret[me] = outb[me]
+
+    @pl.loop(0, 8)
+    def _(i):
+        at = pl.ds(pl.multiple_of(i * 128, 128), 128)
+        tb[at, :] = jnp.transpose(arr[:, :, at].reshape(1024, 128))
+
+    @pl.loop(0, 4)
+    def _(i):
+        rows = pl.ds(pl.multiple_of(i * 256, 256), 256)
+        for side in (0, 1):
+            if side == 0:
+                gram = jnp.dot(tb[rows, :], arr[...].reshape(1024, 1024), preferred_element_type=F32)
+            else:
+                gram = jnp.dot(arr[pl.ds(i * 8, 8)].reshape(256, 1024), tb[...], preferred_element_type=F32)
+            stat_in(i, side).wait()
+            old = st[side]
+            new = jnp.where(mine == 1, 0.9 * old + 0.1 * gram, old)
+
+            @pl.when(i > 0)
+            def _():
+                stat_out(i - 1, side).wait()
+
+            so[side] = new
+            stat_out(i, side).start()
+
+            @pl.when(i < 3)
+            def _():
+                stat_in(i + 1, side).start()
+
+    @pl.loop(1, 32)
+    def _(k):
+        back(k)[1].wait()
+
+    for r in range(14):
+        update[0, :, r * 1024 : (r + 1) * 1024] = ret[owner_of[r]]
+    for side in (0, 1):
+        stat_out(3, side).wait()
+
+
+def step(emb, hid, eg, hg, cot, own, lstat, rstat, lroot, rroot):
     dma = pltpu.SemaphoreType.DMA
+    vmem = pl.BlockSpec(memory_space=pltpu.VMEM)
+    hbm = pl.BlockSpec(memory_space=pl.ANY)
     return pl.pallas_call(
         reduce_kernel,
-        out_shape=jax.ShapeDtypeStruct((32, 2 * WIDTH), BF16),
-        in_specs=[pl.BlockSpec(memory_space=pltpu.VMEM)] * 5,
-        out_specs=pl.BlockSpec(memory_space=pltpu.VMEM),
+        out_shape=(
+            jax.ShapeDtypeStruct((1024, 1024), F32),
+            jax.ShapeDtypeStruct((1024, 1024), F32),
+            jax.ShapeDtypeStruct((1, 32, 2 * WIDTH), BF16),
+        ),
+        in_specs=[vmem] * 5 + [pl.BlockSpec(memory_space=pltpu.SMEM)] + [hbm] * 4,
+        out_specs=(hbm, hbm, vmem),
         scratch_shapes=[
             pltpu.VMEM((4, 2, 4, 4, 64, 256), BF16),
             pltpu.VMEM((2, 256, PART), BF16),
@@ -266,18 +403,27 @@
             pltpu.VMEM((2, 8, 256), F32),
             pltpu.VMEM((2, 4, 4, 4, 64, HALF), BF16),
             pltpu.VMEM((2, 4, 6, 2, 64, HALF), BF16),
-            pltpu.VMEM((2, 4, 4, 64, HALF), BF16),
             pltpu.VMEM((2, 4, 6, 32, HALF), BF16),
             pltpu.VMEM((4, 2, 32, PART), BF16),
             pltpu.VMEM((8, 32, PART), BF16),
+            pltpu.VMEM((14, 32, 1024), BF16),
+            pltpu.VMEM((32, 32, 1024), BF16),
+            pltpu.VMEM((32, 32, 1024), BF16),
+            pltpu.VMEM((32, 32, 1024), BF16),
+            pltpu.VMEM((1024, 1024), BF16),
+            pltpu.VMEM((1024, 1024), BF16),
+            pltpu.VMEM((1024, 1024), BF16),
+            pltpu.VMEM((2, 256, 1024), F32),
+            pltpu.VMEM((2, 256, 1024), F32),
             dma((3,)), dma((3,)), dma((2,)), dma((2,)), dma((3,)), dma((3,)), dma((4,)), dma((4,)),
-            dma((2, 4, 6)), dma((2, 4, 6)), dma((2, 4, 6)), dma((2, 4, 6)), dma((4, 2)), dma((4, 2)), dma((2,)),
+            dma((2, 4, 6)), dma((2, 4, 6)), dma((2, 4, 6)), dma((2, 4, 6)), dma((4, 2)), dma((4, 2)), dma((4,)),
+            dma((32,)), dma((32,)), dma((32,)), dma((32,)), dma((2,)), dma((2,)),
         ],
         compiler_params=pltpu.CompilerParams(
-            collective_id=0, has_side_effects=True, vmem_limit_bytes=60 * 2**20
+            collective_id=0, has_side_effects=True, vmem_limit_bytes=62 * 2**20
         ),
-        name="reduce_share",
-    )(emb, hid, eg, hg, cot)
+        name="shampoo",
+    )(emb, hid, eg, hg, cot, own, lstat, rstat, lroot, rroot)
 
 
 def body(
@@ -292,47 +438,10 @@
     right_root,
     owners,
 ):
-    share = reduced_share(embedding, hidden, embed_gain[None], hidden_gain[None], cotangent)
-    total_in = share.shape[1]
-    replicas = lax.axis_size("dp")
-    side = cotangent.shape[1]
-    sliver = side // replicas
-    block_rows = total_in // side
-    my_replica = lax.axis_index("dp")
-    my_column = lax.axis_index("mp")
-    column_owners = lax.dynamic_index_in_dim(owners, my_column, 0, keepdims=False)
-    owner_hot = (column_owners[None, :] == jnp.arange(replicas, dtype=jnp.int32)[:, None]).astype(
-        jnp.bfloat16
+    return step(
+        embedding, hidden, embed_gain[None], hidden_gain[None], cotangent, owners,
+        left_stat, right_stat, left_root, right_root,
     )
-    pieces = share.reshape(sliver, block_rows, side)
-    outgoing = jnp.einsum(
-        "or,srb->osb", owner_hot, pieces, preferred_element_type=jnp.float32
-    ).astype(jnp.bfloat16)
-    arrived = lax.all_to_all(outgoing, "dp", split_axis=0, concat_axis=1, tiled=True)
-    grad_t = arrived.reshape(side, side)
-    owned = jnp.any(column_owners == my_replica)
-    gram_left = lax.dot_general(
-        grad_t, grad_t, (((0,), (0,)), ((), ())), preferred_element_type=jnp.float32
-    )
-    gram_right = lax.dot_general(
-        grad_t, grad_t, (((1,), (1,)), ((), ())), preferred_element_type=jnp.float32
-    )
-    left_new = jnp.where(owned, 0.9 * left_stat + 0.1 * gram_left, left_stat)
-    right_new = jnp.where(owned, 0.9 * right_stat + 0.1 * gram_right, right_stat)
-    inner_t = lax.dot_general(
-        right_root, grad_t, (((0,), (0,)), ((), ())), preferred_element_type=jnp.float32
-    ).astype(jnp.bfloat16)
-    result_t = lax.dot_general(
-        inner_t, left_root, (((1,), (1,)), ((), ())), preferred_element_type=jnp.float32
-    ).astype(jnp.bfloat16)
-    returned = lax.all_to_all(
-        result_t.reshape(replicas, sliver, side), "dp", split_axis=0, concat_axis=0, tiled=True
-    )
-    placed = jnp.einsum(
-        "or,osb->srb", owner_hot, returned, preferred_element_type=jnp.float32
-    ).astype(jnp.bfloat16)
-    update = placed.reshape(1, sliver, total_in)
-    return (left_new, right_new, update)
 
 
 def solution(mesh):

time: 198 us -> 191 us (0.965); the launches traced: 198 us -> 188 us
  Pallas kernels: 109 us -> 177 us
  blocking collectives: 34 us -> 0 us
  matrix products: 26.4 us -> 0 us
  waiting for transfers between devices: 14.3 us -> 0 us
  starting transfers between devices: 4.76 us -> 0 us
  local copies, waits for them, and re-layouts: 7.54 us -> 10.5 us
    pallas_call x1, Pallas kernels: 109 us -> 177 us  [step(): pl.pallas_call(reduce_kernel, out_shape=(jax.ShapeDtypeStruct((1024, 1024...]
    all_to_all x1 -> x0, blocking collectives: 34 us -> none  [body(): lax.all_to_all(outgoing, 'dp', split_axis=0, concat_axis=1, tiled=True)]
    dot_general x5 -> x0, matrix products: 26.4 us -> none  [the longest x1 9.25 us: body(): lax.dot_general(grad_t, grad_t, (((1,), (1,)), ((), ())), preferred_eleme...]
    all_to_all x1 -> x0, waiting for transfers between devices: 14.3 us -> none  [body(): lax.all_to_all(result_t.reshape(replicas, sliver, side), 'dp', split_axis...]
    unnamed x6 -> x7, local copies, waits for them, and re-layouts: 0.02 us -> 7.88 us
    all_to_all x1 -> x0, starting transfers between devices: 4.76 us -> none  [body(): lax.all_to_all(result_t.reshape(replicas, sliver, side), 'dp', split_axis...]
    reshape x2 -> x0, local copies, waits for them, and re-layouts: 3.63 us -> none  [the longest x1 1.92 us: body(): pieces = share.reshape(sliver, block_rows, side)]
  transfers between devices with their start and end apart: 1 -> 0, of which waited for: 1 -> 0; matrix products, arithmetic and copies ran while one was open for 7% -> 0% of each run, Pallas kernels for 0% -> 0%
where the time goes in v2:
time: 191 us; the launch traced here: 188 us
  Pallas kernels  177 us (93%)
  local copies, waits for them, and re-layouts  10.5 us (5%)
    pallas_call x1, Pallas kernels, step(): pl.pallas_call(reduce_kernel, out_shape=(jax.ShapeDtypeStruct((1024, 1024...  177 us
    unnamed x7, local copies, waits for them, and re-layouts  7.88 us

profile of v2, /device:TPU:8, one launch (start us, length us, event | category | flops | bytes accessed | tf_op | source)
XLA Modules:
  0.0 188.0 jit_solution(1765749550993894977)
XLA Ops:
  0.6 1.3 broadcast_in_dim.6.eg
  1.9 1.3 broadcast_in_dim.7.hg
  3.2 176.9 %shampoo.1 = (f32[1024,1024]{1,0:T(8,128)}, f32[1024,1024]{1,0:T(8,128)}, bf16[1,32,14336]{2,1,0:T(8,128)(2,1)}) custom-call(bf16[256,1792]{1,0:T(8,128)(2,1)} %emb.1, bf16[256,1792]{1,0:T(8,128)(2,1)} %hid.1, f32[1,1792]{1,0:T(1,128)} %broadcast_in_dim.6.eg, f32[1,1792]{1,0:T(1,128)} %broadcast_in_dim.7.hg, bf16[256,1024]{1,0:T(8,128)(2,1)} %cot.1, ...), custom_call_target="tpu_custom_call" | custom-call | tf_op jit(solution)/shard_map/shampoo/pallas_call | solution.py:390
  180.1 0.0 copy-start
  180.1 4.9 %copy.16 = f32[1024,1024]{1,0:T(8,128)} copy(f32[1024,1024]{1,0:T(8,128)} %get-tuple-element.6) | data formatting | bytes 8388608
  185.1 0.0 copy-done
  185.1 0.0 copy-start.1
  185.1 2.0 %copy.17 = f32[1024,1024]{1,0:T(8,128)} copy(f32[1024,1024]{1,0:T(8,128)S(1)} %copy-done) | data formatting | bytes 8388608
  187.1 0.0 copy-done.1
  187.1 0.9 copy.18
Async XLA Ops:
  180.1 5.0 %copy-start = (f32[1024,1024]{1,0:T(8,128)S(1)}, f32[1024,1024]{1,0:T(8,128)}, u32[]{:S(2)}) copy-start(f32[1024,1024]{1,0:T(8,128)} %get-tuple-element.7) | copy-start | bytes 12582916
  185.1 2.0 %copy-start.1 = (bf16[1,32,14336]{2,1,0:T(8,128)(2,1)S(1)}, bf16[1,32,14336]{2,1,0:T(8,128)(2,1)}, u32[]{:S(2)}) copy-start(bf16[1,32,14336]{2,1,0:T(8,128)(2,1)} %get-tuple-element.8) | copy-start | bytes 2752516

commit v3 on v2

v3 whole, which is shorter than its diff:
```python
import functools

import jax
import jax.numpy as jnp
from jax import lax
from jax.experimental import pallas as pl
from jax.experimental.pallas import tpu as pltpu
from jax.sharding import PartitionSpec as P

MESH = pl.DeviceIdType.MESH
F32 = jnp.float32
BF16 = jnp.bfloat16
WIDTH = 7168
PART = 1792
HALF = 896
DELTAS = (0, 1, 3, 2)


def coords():
    dp = lax.axis_index("dp")
    return dp // 8, lax.axis_index("mp"), (dp // 2) % 4, dp % 2


def device(x, y, z, core):
    return ((x * 4 + z) * 2 + core, y)


def remote(src, dst, send, recv, dest):
    return pltpu.make_async_remote_copy(
        src_ref=src, dst_ref=dst, send_sem=send, recv_sem=recv, device_id=dest, device_id_type=MESH
    )


def row_squares(ref):
    acc = jnp.zeros((256, 128), F32)
    for i in range(PART // 128):
        v = ref[:, i * 128 : (i + 1) * 128].astype(F32)
        acc = acc + v * v
    return jnp.sum(jnp.transpose(acc), axis=0, keepdims=True)


def reduce_kernel(
    emb, hid, eg, hg, cot, own, lstat, rstat, lroot, rroot, lnew, rnew, update,
    ct, nb, sq, sc, part, r1, r2, yb, sh, blocks, outb, arr, ret, tb, rt, lt, st, so,
    sq_s, sq_r, sib_s, sib_r, ct_s, ct_r, rel_s, rel_r, p1_s, p1_r, p2_s, p2_r, y_s, y_r, loc,
    o_s, o_r, b_s, b_r, st_i, st_o,
):
    x, y, z, core = coords()
    sib = device(x, y, z, 1 - core)
    nbr = {
        "x": (device((x + 1) % 4, y, z, core), device((x + 3) % 4, y, z, core), x),
        "z": (device(x, y, (z + 1) % 4, core), device(x, y, (z + 3) % 4, core), z),
    }
    barrier = pltpu.get_barrier_semaphore()
    me = (x * 4 + z) * 2 + core

    def peer_of(k):
        tx, tz, tc = (x + k // 8) % 4, (z + (k // 2) % 4) % 4, (core + k % 2) % 2
        return (tx * 4 + tz) * 2 + tc

    for d in (1, 2, 3):
        for c in (core, 1 - core):
            pl.semaphore_signal(barrier, inc=1, device_id=device(x, (y + d) % 4, z, c), device_id_type=MESH)

    for peer in (sib, *nbr["x"][:2], *nbr["z"][:2]):
        pl.semaphore_signal(barrier, inc=1, device_id=peer, device_id_type=MESH)

    r_cp = pltpu.make_async_copy(rroot, tb, loc.at[2])
    r_cp.start()

    ct[0, core] = jnp.transpose(cot[...]).reshape(4, 4, 64, 256)
    sq[core, 0] = jnp.concatenate([row_squares(emb), row_squares(hid), jnp.zeros((6, 256), F32)], axis=0)
    pl.semaphore_wait(barrier, 11)

    sends = []

    def go(cp):
        cp.start()
        sends.append(cp)
        return cp

    sq_cp = [
        go(remote(sq.at[core, 0], sq.at[core, i], sq_s.at[rel, i], sq_r.at[rel, i],
                  device(x, (y + i) % 4, z, (core + rel) % 2)))
        for i in range(4) for rel in (0, 1) if (i, rel) != (0, 0)
    ]
    ct_cp = {}
    rel_cp = {}
    rel_cp[0] = go(remote(ct.at[0, core], ct.at[0, core], rel_s.at[0], rel_r.at[0], sib))

    def along_y(s):
        ct_cp[s] = go(
            remote(ct.at[0, core], ct.at[s, core], ct_s.at[s - 1], ct_r.at[s - 1],
                   device(x, (y + 4 - DELTAS[s]) % 4, z, core))
        )

    along_y(1)
    along_y(2)
    n_cp = remote(emb, nb.at[core], sib_s.at[0], sib_r.at[0], sib)
    l_cp = pltpu.make_async_copy(emb, nb.at[core], loc.at[0])

    @pl.when(core == 0)
    def _():
        remote(hid, nb.at[core], sib_s.at[0], sib_r.at[0], sib).start()
        pltpu.make_async_copy(emb, nb.at[core], loc.at[0]).start()

    @pl.when(core == 1)
    def _():
        remote(emb, nb.at[core], sib_s.at[0], sib_r.at[0], sib).start()
        pltpu.make_async_copy(hid, nb.at[core], loc.at[0]).start()

    sends.append(n_cp)
    gain = jnp.where(core == 0, eg[...], hg[...]).reshape(1, PART)
    for cp in sq_cp:
        cp.wait_recv()
    sc[...] = lax.rsqrt((sq[:, 0] + sq[:, 1] + sq[:, 2] + sq[:, 3]) / WIDTH + 1e-6)
    l_cp.wait()
    n_cp.wait_recv()
    rel_cp[0].wait_recv()
    scale = [jnp.where(core == 0, sc[t, 0:1], sc[t, 1:2]) for t in (0, 1)]

    def relay(s):
        ct_cp[s].wait_recv()
        rel_cp[s] = go(remote(ct.at[s, core], ct.at[s, core], rel_s.at[s], rel_r.at[s], sib))

    axes = (("x", "z"), ("z", "x"))
    cps = {}

    def ring1(ab, s, u, which=range(6)):
        plus, minus, pos = nbr[axes[ab][0]]
        p1, m1, m2 = (pos + 1) % 4, (pos + 3) % 4, (pos + 2) % 4
        src = part.at[ab, u, s]

        def cp(i, ref, dest):
            return remote(ref, r1.at[ab, u, s, i], p1_s.at[ab, u, s, i], p1_r.at[ab, u, s, i], dest)

        parts = (
            (m2, slice(0, 2), plus), (m2, slice(2, 4), minus),
            (p1, slice(2, 4), plus), (m1, slice(0, 2), minus),
            (p1, slice(0, 2), plus), (m1, slice(2, 4), minus),
        )
        return [cp(w, src.at[parts[w][0], parts[w][1]], parts[w][2]) for w in which], (pos, p1, m1)

    def ring2(ab, s, u):
        plus, minus, pos = nbr[axes[ab][1]]
        p1, m1, m2 = (pos + 1) % 4, (pos + 3) % 4, (pos + 2) % 4
        src = part.at[ab, u, s, nbr[axes[ab][0]][2]]

        def cp(i, ref, dest):
            return remote(ref, r2.at[ab, u, s, i], p2_s.at[ab, u, s, i], p2_r.at[ab, u, s, i], dest)

        return [
            cp(0, src.at[m2, 0:16], plus),
            cp(1, src.at[m2, 16:32], minus),
            cp(2, src.at[p1, 16:32], plus),
            cp(3, src.at[m1, 0:16], minus),
            cp(4, src.at[p1, 0:16], plus),
            cp(5, src.at[m1, 16:32], minus),
        ], (pos, p1, m1)

    def product(s):
        if s > 0:
            rel_cp[s].wait_recv()

        @pl.loop(0, 4)
        def _(i):
            g = lax.rem(6 - i, 4)
            xg = lax.rem(x + g, 4)
            zg = lax.rem(z + g, 4)

            def lhs(t, ab):
                v = ct[s, t, xg] if ab == 0 else ct[s, t, :, zg]
                return (v.reshape(256, 256).astype(F32) * scale[t]).astype(BF16)

            for ab, at in ((0, xg), (1, zg)):
                lanes = slice(ab * HALF, (ab + 1) * HALF)
                acc = jnp.dot(lhs(0, ab), nb[0, :, lanes], preferred_element_type=F32)
                acc = acc + jnp.dot(lhs(1, ab), nb[1, :, lanes], preferred_element_type=F32)
                res = acc.astype(BF16).reshape(4, 2, 2, 16, HALF)
                for u in (0, 1):
                    part[ab, u, s, at] = res[:, :, u].reshape(4, 32, HALF)

            for turn, which in ((0, (0, 1)), (1, (2,)), (3, (3,))):

                @pl.when(i == turn)
                def _():
                    for ab in (0, 1):
                        for c in ring1(ab, s, 0, which)[0]:
                            c.start()

    def add(a, *rest):
        out = a.astype(F32)
        for r in rest:
            out = out + r.astype(F32)
        return out

    def stage_a(s, u):
        if u == 0:
            product(s)
        for ab in (0, 1):
            cps[1, ab, s, u] = ring1(ab, s, u)
            for i in range(4):
                if u == 0:
                    sends.append(cps[1, ab, s, u][0][i])
                else:
                    go(cps[1, ab, s, u][0][i])

    def stage_b(s, u):
        for ab in (0, 1):
            c, (pos, p1, m1) = cps[1, ab, s, u]
            c[0].wait_recv()
            part[ab, u, s, p1, 0:2] = add(part[ab, u, s, p1, 0:2], r1[ab, u, s, 0]).astype(BF16)
            go(c[4])
            c[1].wait_recv()
            part[ab, u, s, m1, 2:4] = add(part[ab, u, s, m1, 2:4], r1[ab, u, s, 1]).astype(BF16)
            go(c[5])

    def stage_c(s, u):
        for ab in (0, 1):
            c, (pos, p1, m1) = cps[1, ab, s, u]
            for i in (2, 3, 4, 5):
                c[i].wait_recv()
            part[ab, u, s, pos, 0:2] = add(
                part[ab, u, s, pos, 0:2], r1[ab, u, s, 4], r1[ab, u, s, 3]
            ).astype(BF16)
            part[ab, u, s, pos, 2:4] = add(
                part[ab, u, s, pos, 2:4], r1[ab, u, s, 2], r1[ab, u, s, 5]
            ).astype(BF16)
            cps[2, ab, s, u] = ring2(ab, s, u)
            for i in range(4):
                go(cps[2, ab, s, u][0][i])

    def stage_d(s, u):
        for ab in (0, 1):
            c, (pos, p1, m1) = cps[2, ab, s, u]
            o = nbr[axes[ab][0]][2]
            c[0].wait_recv()
            part[ab, u, s, o, p1, 0:16] = add(part[ab, u, s, o, p1, 0:16], r2[ab, u, s, 0]).astype(BF16)
            go(c[4])
            c[1].wait_recv()
            part[ab, u, s, o, m1, 16:32] = add(part[ab, u, s, o, m1, 16:32], r2[ab, u, s, 1]).astype(BF16)
            go(c[5])

    y_cp = {}

    def stage_e(s, u):
        for ab in (0, 1):
            c, (pos, p1, m1) = cps[2, ab, s, u]
            o = nbr[axes[ab][0]][2]
            for i in (2, 3, 4, 5):
                c[i].wait_recv()
            lanes = slice(ab * HALF, (ab + 1) * HALF)
            g = gain[:, lanes]
            for to, more in ((0, (4, 3)), (1, (2, 5))):
                yb[u, s, to, :, lanes] = (
                    add(part[ab, u, s, o, pos, 16 * to : 16 * to + 16], *[r2[ab, u, s, m] for m in more]) * g
                ).astype(BF16)
        for rel in (0, 1):
            to = (core + rel) % 2
            if s == 0 and rel == 0:
                cp = pltpu.make_async_copy(yb.at[u, s, to], sh.at[u, core * 4 + y], loc.at[u])
                cp.start()
            else:
                cp = go(
                    remote(yb.at[u, s, to], sh.at[u, core * 4 + y], y_s.at[u, s, rel], y_r.at[u, s, rel],
                           device(x, (y + DELTAS[s]) % 4, z, to))
                )
            y_cp[u, s, rel] = cp

    def transpose_root(out):
        @pl.loop(0, 8)
        def _(i):
            at = pl.ds(pl.multiple_of(i * 128, 128), 128)
            out[at, :] = jnp.transpose(tb[:, at])

    def stat_in(i, side):
        rows = pl.ds(pl.multiple_of(i * 128, 128), 128)
        return pltpu.make_async_copy((lstat, rstat)[side].at[rows], st.at[side], st_i.at[side])

    def stat_out(i, side):
        rows = pl.ds(pl.multiple_of(i * 128, 128), 128)
        return pltpu.make_async_copy(so.at[side], (lnew, rnew)[side].at[rows], st_o.at[side])

    owner_of = [own[y, r] for r in range(14)]

    def row_of(d):
        row = jnp.int32(0)
        for r in range(14):
            row = jnp.where(owner_of[r] == d, jnp.int32(r), row)
        return row

    def to_owner(k, u):
        t = peer_of(k)
        return t, remote(outb.at[t, u], arr.at[me, u], o_s.at[u, k], o_r.at[u, k], (t, y))

    def back(k):
        t = peer_of(k)
        return t, remote(outb.at[t], ret.at[me], b_s.at[k], b_r.at[k], (t, y))

    def send_owners(u):
        for s in range(4):
            for rel in (0, 1):
                if s == 0 and rel == 0:
                    y_cp[u, s, rel].wait()
                else:
                    y_cp[u, s, rel].wait_recv()
        for r in range(14):
            at = r * 1024
            done = 0
            while done < 1024:
                i, lane = (at + done) // PART, (at + done) % PART
                size = min(1024 - done, PART - lane)
                blocks[u, r, :, done : done + size] = sh[u, i, :, lane : lane + size]
                done += size

        @pl.loop(1, 32)
        def _(k):
            t, cp = to_owner(k, u)
            outb[t, u] = blocks[u, row_of(t)]
            cp.start()

        arr[me, u] = blocks[u, row_of(me)]

    chunks = ((0, 0), (0, 1), (1, 0), (2, 0), (3, 0), (1, 1), (2, 1), (3, 1))
    for turn in range(12):
        for behind, stage in enumerate((stage_a, stage_b, stage_c, stage_d, stage_e)):
            if 0 <= turn - behind < 8:
                stage(*chunks[turn - behind])
        if 1 <= turn <= 3:
            relay(turn)
        if turn == 1:
            along_y(3)
        if turn == 4:
            r_cp.wait()
            transpose_root(rt)
            l_root = pltpu.make_async_copy(lroot, tb, loc.at[3])
            l_root.start()
        if turn == 5:
            l_root.wait()
            transpose_root(lt)
            stat_in(0, 0).start()
            stat_in(0, 1).start()
        if turn == 8:
            send_owners(0)
    send_owners(1)
    mine = jnp.int32(0)
    for r in range(14):
        mine = jnp.where(owner_of[r] == me, jnp.int32(1), mine)
    for cp in sends:
        cp.wait_send()

    @pl.loop(1, 32)
    def _(k):
        for u in (0, 1):
            to_owner(k, u)[1].wait()

    @pl.loop(0, 4)
    def _(i):
        g = lax.rem(i + 1, 4)
        tx = lax.rem(x + g, 4)
        rows = pl.ds(pl.multiple_of(tx * 256, 256), 256)
        inner = jnp.dot(
            rt[rows, :], arr[...].reshape(1024, 1024), preferred_element_type=F32
        ).astype(BF16)
        res = jnp.dot(inner, lt[...], preferred_element_type=F32).astype(BF16)
        outb[pl.ds(tx * 8, 8)] = res.reshape(8, 2, 16, 1024)
        for j in range(8):
            k = g * 8 + j

            @pl.when(k > 0)
            def _():
                back(k)[1].start()

    ret[me] = outb[me]

    @pl.loop(0, 8)
    def _(i):
        at = pl.ds(pl.multiple_of(i * 128, 128), 128)
        tb[at, :] = jnp.transpose(arr[:, :, :, at].reshape(1024, 128))

    @pl.loop(0, 8)
    def _(i):
        rows = pl.ds(pl.multiple_of(i * 128, 128), 128)
        for side in (0, 1):
            if side == 0:
                gram = jnp.dot(tb[rows, :], arr[...].reshape(1024, 1024), preferred_element_type=F32)
            else:
                gram = jnp.dot(arr[pl.ds(i * 4, 4)].reshape(128, 1024), tb[...], preferred_element_type=F32)
            stat_in(i, side).wait()
            old = st[side]
            new = jnp.where(mine == 1, 0.9 * old + 0.1 * gram, old)

            @pl.when(i > 0)
            def _():
                stat_out(i - 1, side).wait()

            so[side] = new
            stat_out(i, side).start()

            @pl.when(i < 7)
            def _():
                stat_in(i + 1, side).start()

    @pl.loop(1, 32)
    def _(k):
        back(k)[1].wait()

    for r in range(14):
        update[0, :, r * 1024 : (r + 1) * 1024] = ret[owner_of[r]].reshape(32, 1024)
    for side in (0, 1):
        stat_out(7, side).wait()


def step(emb, hid, eg, hg, cot, own, lstat, rstat, lroot, rroot):
    dma = pltpu.SemaphoreType.DMA
    vmem = pl.BlockSpec(memory_space=pltpu.VMEM)
    hbm = pl.BlockSpec(memory_space=pl.ANY)
    return pl.pallas_call(
        reduce_kernel,
        out_shape=(
            jax.ShapeDtypeStruct((1024, 1024), F32),
            jax.ShapeDtypeStruct((1024, 1024), F32),
            jax.ShapeDtypeStruct((1, 32, 2 * WIDTH), BF16),
        ),
        in_specs=[vmem] * 5 + [pl.BlockSpec(memory_space=pltpu.SMEM)] + [hbm] * 4,
        out_specs=(hbm, hbm, vmem),
        scratch_shapes=[
            pltpu.VMEM((4, 2, 4, 4, 64, 256), BF16),
            pltpu.VMEM((2, 256, PART), BF16),
            pltpu.VMEM((2, 4, 8, 256), F32),
            pltpu.VMEM((2, 8, 256), F32),
            pltpu.VMEM((2, 2, 4, 4, 4, 32, HALF), BF16),
            pltpu.VMEM((2, 2, 4, 6, 2, 32, HALF), BF16),
            pltpu.VMEM((2, 2, 4, 6, 16, HALF), BF16),
            pltpu.VMEM((2, 4, 2, 16, PART), BF16),
            pltpu.VMEM((2, 8, 16, PART), BF16),
            pltpu.VMEM((2, 14, 16, 1024), BF16),
            pltpu.VMEM((32, 2, 16, 1024), BF16),
            pltpu.VMEM((32, 2, 16, 1024), BF16),
            pltpu.VMEM((32, 2, 16, 1024), BF16),
            pltpu.VMEM((1024, 1024), BF16),
            pltpu.VMEM((1024, 1024), BF16),
            pltpu.VMEM((1024, 1024), BF16),
            pltpu.VMEM((2, 128, 1024), F32),
            pltpu.VMEM((2, 128, 1024), F32),
            dma((2, 4)), dma((2, 4)), dma((1,)), dma((1,)), dma((3,)), dma((3,)), dma((4,)), dma((4,)),
            dma((2, 2, 4, 6)), dma((2, 2, 4, 6)), dma((2, 2, 4, 6)), dma((2, 2, 4, 6)),
            dma((2, 4, 2)), dma((2, 4, 2)), dma((4,)),
            dma((2, 32)), dma((2, 32)), dma((32,)), dma((32,)), dma((2,)), dma((2,)),
        ],
        compiler_params=pltpu.CompilerParams(
            collective_id=0, has_side_effects=True, vmem_limit_bytes=62 * 2**20
        ),
        name="shampoo",
    )(emb, hid, eg, hg, cot, own, lstat, rstat, lroot, rroot)


def body(
    embedding,
    hidden,
    embed_gain,
    hidden_gain,
    cotangent,
    left_stat,
    right_stat,
    left_root,
    right_root,
    owners,
):
    return step(
        embedding, hidden, embed_gain, hidden_gain, cotangent, owners,
        left_stat, right_stat, left_root, right_root,
    )


def solution(mesh):
    placed = (
        P("dp", "mp"),
        P("dp", "mp"),
        P("mp"),
        P("mp"),
        P("dp", "mp"),
        P("dp", "mp"),
        P("dp", "mp"),
        P("dp", "mp"),
        P("dp", "mp"),
        P(),
    )
    return jax.shard_map(
        body,
        mesh=mesh,
        in_specs=placed,
        out_specs=(P("dp", "mp"), P("dp", "mp"), P("mp", "dp", None)),
        check_vma=False,
    )
```

time: 191 us -> 178 us (0.932)
  Pallas kernels: 177 us -> 167 us
  local copies, waits for them, and re-layouts: 10.5 us -> 7.88 us
    pallas_call x1, Pallas kernels: 177 us -> 167 us  [step(): pl.pallas_call(reduce_kernel, out_shape=(jax.ShapeDtypeStruct((1024, 1024...]
    broadcast_in_dim x2 -> x0, local copies, waits for them, and re-layouts: 2.59 us -> none  [the longest x1 1.3 us: body(): embed_gain[None]]
where the time goes in v3:
time: 178 us; the launch traced here: 175 us
  Pallas kernels  167 us (94%)
  local copies, waits for them, and re-layouts  7.88 us (4%)
    pallas_call x1, Pallas kernels, step(): pl.pallas_call(reduce_kernel, out_shape=(jax.ShapeDtypeStruct((1024, 1024...  167 us
    unnamed x7, local copies, waits for them, and re-layouts  7.88 us

profile of v3, /device:TPU:8, one launch (start us, length us, event | category | flops | bytes accessed | tf_op | source)
XLA Modules:
  0.0 175.2 jit_solution(2967453942708089613)
XLA Ops:
  0.6 166.6 %shampoo.1 = (f32[1024,1024]{1,0:T(8,128)}, f32[1024,1024]{1,0:T(8,128)}, bf16[1,32,14336]{2,1,0:T(8,128)(2,1)}) custom-call(bf16[256,1792]{1,0:T(8,128)(2,1)} %emb.1, bf16[256,1792]{1,0:T(8,128)(2,1)} %hid.1, f32[1792]{0:T(1024)} %eg.1, f32[1792]{0:T(1024)} %hg.1, bf16[256,1024]{1,0:T(8,128)(2,1)} %cot.1, s32[4,14]{1,0:T(4,128)} %own.1, ...), custom_call_target="tpu_custom_call" | custom-call | tf_op jit(solution)/shard_map/shampoo/pallas_call | solution.py:418
  167.3 0.0 copy-start
  167.3 4.9 %copy.16 = f32[1024,1024]{1,0:T(8,128)} copy(f32[1024,1024]{1,0:T(8,128)} %get-tuple-element.6) | data formatting | bytes 8388608
  172.2 0.0 copy-done
  172.2 0.0 copy-start.1
  172.2 2.0 %copy.17 = f32[1024,1024]{1,0:T(8,128)} copy(f32[1024,1024]{1,0:T(8,128)S(1)} %copy-done) | data formatting | bytes 8388608
  174.2 0.0 copy-done.1
  174.2 0.9 copy.18
Async XLA Ops:
  167.3 5.0 %copy-start = (f32[1024,1024]{1,0:T(8,128)S(1)}, f32[1024,1024]{1,0:T(8,128)}, u32[]{:S(2)}) copy-start(f32[1024,1024]{1,0:T(8,128)} %get-tuple-element.7) | copy-start | bytes 12582916
  172.2 2.0 %copy-start.1 = (bf16[1,32,14336]{2,1,0:T(8,128)(2,1)S(1)}, bf16[1,32,14336]{2,1,0:T(8,128)(2,1)}, u32[]{:S(2)}) copy-start(bf16[1,32,14336]{2,1,0:T(8,128)(2,1)} %get-tuple-element.8) | copy-start | bytes 2752516

commit v4 on v3

--- a/solution.py
+++ b/solution.py
@@ -41,9 +41,9 @@
 
 def reduce_kernel(
     emb, hid, eg, hg, cot, own, lstat, rstat, lroot, rroot, lnew, rnew, update,
-    ct, nb, sq, sc, part, r1, r2, yb, sh, blocks, outb, arr, ret, tb, rt, lt, st, so,
+    ct, nb, sq, sc, part, r1, r2, yb, sh, blocks, outb, arr, ret, tb, rt, lt, st, so, mid, midb,
     sq_s, sq_r, sib_s, sib_r, ct_s, ct_r, rel_s, rel_r, p1_s, p1_r, p2_s, p2_r, y_s, y_r, loc,
-    o_s, o_r, b_s, b_r, st_i, st_o,
+    o_s, o_r, q_s, q_r, b_s, b_r, c_s, c_r, st_i, st_o,
 ):
     x, y, z, core = coords()
     sib = device(x, y, z, 1 - core)
@@ -53,10 +53,6 @@
     }
     barrier = pltpu.get_barrier_semaphore()
     me = (x * 4 + z) * 2 + core
-
-    def peer_of(k):
-        tx, tz, tc = (x + k // 8) % 4, (z + (k // 2) % 4) % 4, (core + k % 2) % 2
-        return (tx * 4 + tz) * 2 + tc
 
     for d in (1, 2, 3):
         for c in (core, 1 - core):
@@ -289,13 +285,60 @@
             row = jnp.where(owner_of[r] == d, jnp.int32(r), row)
         return row
 
-    def to_owner(k, u):
-        t = peer_of(k)
-        return t, remote(outb.at[t, u], arr.at[me, u], o_s.at[u, k], o_r.at[u, k], (t, y))
-
-    def back(k):
-        t = peer_of(k)
-        return t, remote(outb.at[t], ret.at[me], b_s.at[k], b_r.at[k], (t, y))
+    def line(ab, d):
+        return ((x + d) % 4, z) if ab == 0 else (x, (z + d) % 4)
+
+    def spread(src_of, mid, ab, d, send, recv):
+        tx, tz = line(ab, d)
+        here = x if ab == 0 else z
+        return remote(src_of(ab, tx if ab == 0 else tz), mid.at[here], send, recv, device(tx, y, tz, core))
+
+    def deliver(mid, dst_of, ab, d, dc, send, recv):
+        tx, tz = line(1 - ab, d)
+        tc = (core + dc) % 2
+        return remote(mid.at[:, tz if ab == 0 else tx, tc], dst_of(ab), send, recv, device(tx, y, tz, tc))
+
+    HOPS = [(d, dc) for d in (2, 1, 3, 0) for dc in (0, 1) if (d, dc) != (0, 0)]
+
+    def owner_src(u):
+        def src_of(ab, at):
+            lanes = pl.ds(512 * ab, 512)
+            return outb.at[at, :, :, u, :, lanes] if ab == 0 else outb.at[:, at, :, u, :, lanes]
+
+        return src_of
+
+    def owner_dst(u):
+        def dst_of(ab):
+            lanes = pl.ds(512 * ab, 512)
+            return arr.at[:, z, core, u, :, lanes] if ab == 0 else arr.at[x, :, core, u, :, lanes]
+
+        return dst_of
+
+    def owner_spread(u):
+        return [
+            spread(owner_src(u), mid.at[u, ab], ab, d, o_s.at[u, ab, d], o_r.at[u, ab, d])
+            for d in (2, 1, 3) for ab in (0, 1)
+        ]
+
+    def owner_deliver(u):
+        return [
+            deliver(mid.at[u, ab], owner_dst(u), ab, d, dc, q_s.at[u, ab, d, dc], q_r.at[u, ab, d, dc])
+            for d, dc in HOPS for ab in (0, 1)
+        ]
+
+    def back_src(ab, at):
+        return outb.at[at, :, :, 0] if ab == 0 else outb.at[:, at, :, 1]
+
+    def back_dst(ab):
+        return ret.at[:, z, core, 0] if ab == 0 else ret.at[x, :, core, 1]
+
+    def back_spread(ab, d):
+        return spread(back_src, midb.at[ab], ab, d, b_s.at[ab, d], b_r.at[ab, d])
+
+    def back_deliver(ab, d, dc):
+        return deliver(midb.at[ab], back_dst, ab, d, dc, c_s.at[ab, d, dc], c_r.at[ab, d, dc])
+
+    passing = {}
 
     def send_owners(u):
         for s in range(4):
@@ -313,13 +356,24 @@
                 blocks[u, r, :, done : done + size] = sh[u, i, :, lane : lane + size]
                 done += size
 
-        @pl.loop(1, 32)
-        def _(k):
-            t, cp = to_owner(k, u)
-            outb[t, u] = blocks[u, row_of(t)]
-            cp.start()
-
-        arr[me, u] = blocks[u, row_of(me)]
+        @pl.loop(0, 32)
+        def _(t):
+            outb[t // 8, (t // 2) % 4, t % 2, u] = blocks[u, row_of(t)]
+
+        passing[1, u] = owner_spread(u)
+        for cp in passing[1, u]:
+            go(cp)
+        mid[u, 0, x] = outb[x, :, :, u, :, 0:512]
+        mid[u, 1, z] = outb[:, z, :, u, :, 512:1024]
+
+    def pass_owners(u):
+        for cp in passing[1, u]:
+            cp.wait_recv()
+        passing[2, u] = owner_deliver(u)
+        for cp in passing[2, u]:
+            go(cp)
+        arr[:, z, core, u, :, 0:512] = mid[u, 0, :, z, core]
+        arr[x, :, core, u, :, 512:1024] = mid[u, 1, :, x, core]
 
     chunks = ((0, 0), (0, 1), (1, 0), (2, 0), (3, 0), (1, 1), (2, 1), (3, 1))
     for turn in range(12):
@@ -342,71 +396,91 @@
             stat_in(0, 1).start()
         if turn == 8:
             send_owners(0)
+        if turn == 10:
+            pass_owners(0)
     send_owners(1)
+    pass_owners(1)
     mine = jnp.int32(0)
     for r in range(14):
         mine = jnp.where(owner_of[r] == me, jnp.int32(1), mine)
+    for u in (0, 1):
+        for cp in passing[2, u]:
+            cp.wait_recv()
     for cp in sends:
         cp.wait_send()
 
-    @pl.loop(1, 32)
-    def _(k):
-        for u in (0, 1):
-            to_owner(k, u)[1].wait()
-
     @pl.loop(0, 4)
     def _(i):
-        g = lax.rem(i + 1, 4)
+        g = lax.rem(6 - i, 4)
         tx = lax.rem(x + g, 4)
         rows = pl.ds(pl.multiple_of(tx * 256, 256), 256)
         inner = jnp.dot(
             rt[rows, :], arr[...].reshape(1024, 1024), preferred_element_type=F32
         ).astype(BF16)
         res = jnp.dot(inner, lt[...], preferred_element_type=F32).astype(BF16)
-        outb[pl.ds(tx * 8, 8)] = res.reshape(8, 2, 16, 1024)
-        for j in range(8):
-            k = g * 8 + j
-
-            @pl.when(k > 0)
+        outb[tx] = res.reshape(4, 2, 2, 16, 1024)
+        for turn, d in ((0, 2), (1, 1), (3, 3)):
+
+            @pl.when(i == turn)
             def _():
-                back(k)[1].start()
-
-    ret[me] = outb[me]
+                back_spread(0, d).start()
+
+    for d in (2, 1, 3):
+        back_spread(1, d).start()
+    midb[0, x] = outb[x, :, :, 0]
+    midb[1, z] = outb[:, z, :, 1]
 
     @pl.loop(0, 8)
     def _(i):
         at = pl.ds(pl.multiple_of(i * 128, 128), 128)
-        tb[at, :] = jnp.transpose(arr[:, :, :, at].reshape(1024, 128))
-
-    @pl.loop(0, 8)
-    def _(i):
-        rows = pl.ds(pl.multiple_of(i * 128, 128), 128)
-        for side in (0, 1):
-            if side == 0:
-                gram = jnp.dot(tb[rows, :], arr[...].reshape(1024, 1024), preferred_element_type=F32)
-            else:
-                gram = jnp.dot(arr[pl.ds(i * 4, 4)].reshape(128, 1024), tb[...], preferred_element_type=F32)
-            stat_in(i, side).wait()
-            old = st[side]
-            new = jnp.where(mine == 1, 0.9 * old + 0.1 * gram, old)
-
-            @pl.when(i > 0)
-            def _():
-                stat_out(i - 1, side).wait()
-
-            so[side] = new
-            stat_out(i, side).start()
-
-            @pl.when(i < 7)
-            def _():
-                stat_in(i + 1, side).start()
-
-    @pl.loop(1, 32)
-    def _(k):
-        back(k)[1].wait()
+        for w in range(4):
+            tb[at, w * 256 : (w + 1) * 256] = jnp.transpose(arr[w, :, :, :, :, at].reshape(256, 128))
+
+    def grams(first, last):
+        @pl.loop(first, last)
+        def _(i):
+            rows = pl.ds(pl.multiple_of(i * 128, 128), 128)
+            for side in (0, 1):
+                if side == 0:
+                    gram = jnp.dot(tb[rows, :], arr[...].reshape(1024, 1024), preferred_element_type=F32)
+                else:
+                    mine_rows = arr[i // 2, pl.ds(2 * (i % 2), 2)].reshape(128, 1024)
+                    gram = jnp.dot(mine_rows, tb[...], preferred_element_type=F32)
+                stat_in(i, side).wait()
+                old = st[side]
+                new = jnp.where(mine == 1, 0.9 * old + 0.1 * gram, old)
+
+                @pl.when(i > 0)
+                def _():
+                    stat_out(i - 1, side).wait()
+
+                so[side] = new
+                stat_out(i, side).start()
+
+                @pl.when(i < 7)
+                def _():
+                    stat_in(i + 1, side).start()
+
+    grams(0, 4)
+    for d in (2, 1, 3):
+        for ab in (0, 1):
+            back_spread(ab, d).wait_recv()
+    last = [back_deliver(ab, d, dc) for d, dc in HOPS for ab in (0, 1)]
+    for cp in last:
+        cp.start()
+    ret[:, z, core, 0] = midb[0, :, z, core]
+    ret[x, :, core, 1] = midb[1, :, x, core]
+    grams(4, 8)
+    for cp in last:
+        cp.wait()
+    for d in (2, 1, 3):
+        for ab in (0, 1):
+            back_spread(ab, d).wait_send()
 
     for r in range(14):
-        update[0, :, r * 1024 : (r + 1) * 1024] = ret[owner_of[r]].reshape(32, 1024)
+        update[0, :, r * 1024 : (r + 1) * 1024] = ret[
+            owner_of[r] // 8, (owner_of[r] // 2) % 4, owner_of[r] % 2
+        ].reshape(32, 1024)
     for side in (0, 1):
         stat_out(7, side).wait()
 
@@ -435,18 +509,21 @@
             pltpu.VMEM((2, 4, 2, 16, PART), BF16),
             pltpu.VMEM((2, 8, 16, PART), BF16),
             pltpu.VMEM((2, 14, 16, 1024), BF16),
-            pltpu.VMEM((32, 2, 16, 1024), BF16),
-            pltpu.VMEM((32, 2, 16, 1024), BF16),
-            pltpu.VMEM((32, 2, 16, 1024), BF16),
+            pltpu.VMEM((4, 4, 2, 2, 16, 1024), BF16),
+            pltpu.VMEM((4, 4, 2, 2, 16, 1024), BF16),
+            pltpu.VMEM((4, 4, 2, 2, 16, 1024), BF16),
             pltpu.VMEM((1024, 1024), BF16),
             pltpu.VMEM((1024, 1024), BF16),
             pltpu.VMEM((1024, 1024), BF16),
             pltpu.VMEM((2, 128, 1024), F32),
             pltpu.VMEM((2, 128, 1024), F32),
+            pltpu.VMEM((2, 2, 4, 4, 2, 16, 512), BF16),
+            pltpu.VMEM((2, 4, 4, 2, 16, 1024), BF16),
             dma((2, 4)), dma((2, 4)), dma((1,)), dma((1,)), dma((3,)), dma((3,)), dma((4,)), dma((4,)),
             dma((2, 2, 4, 6)), dma((2, 2, 4, 6)), dma((2, 2, 4, 6)), dma((2, 2, 4, 6)),
             dma((2, 4, 2)), dma((2, 4, 2)), dma((4,)),
-            dma((2, 32)), dma((2, 32)), dma((32,)), dma((32,)), dma((2,)), dma((2,)),
+            dma((2, 2, 4)), dma((2, 2, 4)), dma((2, 2, 4, 2)), dma((2, 2, 4, 2)),
+            dma((2, 4)), dma((2, 4)), dma((2, 4, 2)), dma((2, 4, 2)), dma((2,)), dma((2,)),
         ],
         compiler_params=pltpu.CompilerParams(
             collective_id=0, has_side_effects=True, vmem_limit_bytes=62 * 2**20

time: 178 us -> 171 us (0.961)
  Pallas kernels: 167 us -> 161 us
    pallas_call x1, Pallas kernels: 167 us -> 161 us  [step(): pl.pallas_call(reduce_kernel, out_shape=(jax.ShapeDtypeStruct((1024, 1024...]
where the time goes in v4:
time: 171 us; the launch traced here: 169 us
  Pallas kernels  161 us (94%)
  local copies, waits for them, and re-layouts  7.88 us (5%)
    pallas_call x1, Pallas kernels, step(): pl.pallas_call(reduce_kernel, out_shape=(jax.ShapeDtypeStruct((1024, 1024...  161 us
    unnamed x7, local copies, waits for them, and re-layouts  7.88 us

profile of v4, /device:TPU:8, one launch (start us, length us, event | category | flops | bytes accessed | tf_op | source)
XLA Modules:
  0.0 169.3 jit_solution(14928819877988738635)
XLA Ops:
  0.6 160.7 %shampoo.1 = (f32[1024,1024]{1,0:T(8,128)}, f32[1024,1024]{1,0:T(8,128)}, bf16[1,32,14336]{2,1,0:T(8,128)(2,1)}) custom-call(bf16[256,1792]{1,0:T(8,128)(2,1)} %emb.1, bf16[256,1792]{1,0:T(8,128)(2,1)} %hid.1, f32[1792]{0:T(1024)} %eg.1, f32[1792]{0:T(1024)} %hg.1, bf16[256,1024]{1,0:T(8,128)(2,1)} %cot.1, s32[4,14]{1,0:T(4,128)} %own.1, ...), custom_call_target="tpu_custom_call" | custom-call | tf_op jit(solution)/shard_map/shampoo/pallas_call | solution.py:492
  161.4 0.0 copy-start
  161.4 4.9 %copy.16 = f32[1024,1024]{1,0:T(8,128)} copy(f32[1024,1024]{1,0:T(8,128)} %get-tuple-element.6) | data formatting | bytes 8388608
  166.3 0.0 copy-done
  166.3 0.0 copy-start.1
  166.3 2.0 %copy.17 = f32[1024,1024]{1,0:T(8,128)} copy(f32[1024,1024]{1,0:T(8,128)S(1)} %copy-done) | data formatting | bytes 8388608
  168.3 0.0 copy-done.1
  168.3 0.9 copy.18
Async XLA Ops:
  161.4 5.0 %copy-start = (f32[1024,1024]{1,0:T(8,128)S(1)}, f32[1024,1024]{1,0:T(8,128)}, u32[]{:S(2)}) copy-start(f32[1024,1024]{1,0:T(8,128)} %get-tuple-element.7) | copy-start | bytes 12582916
  166.3 2.0 %copy-start.1 = (bf16[1,32,14336]{2,1,0:T(8,128)(2,1)S(1)}, bf16[1,32,14336]{2,1,0:T(8,128)(2,1)}, u32[]{:S(2)}) copy-start(bf16[1,32,14336]{2,1,0:T(8,128)(2,1)} %get-tuple-element.8) | copy-start | bytes 2752516

commit v5 on v4

--- a/solution.py
+++ b/solution.py
@@ -43,7 +43,7 @@
     emb, hid, eg, hg, cot, own, lstat, rstat, lroot, rroot, lnew, rnew, update,
     ct, nb, sq, sc, part, r1, r2, yb, sh, blocks, outb, arr, ret, tb, rt, lt, st, so, mid, midb,
     sq_s, sq_r, sib_s, sib_r, ct_s, ct_r, rel_s, rel_r, p1_s, p1_r, p2_s, p2_r, y_s, y_r, loc,
-    o_s, o_r, q_s, q_r, b_s, b_r, c_s, c_r, st_i, st_o,
+    o_s, o_r, q_s, q_r, b_s, b_r, c_s, c_r, t_s, t_r, st_i, st_o,
 ):
     x, y, z, core = coords()
     sib = device(x, y, z, 1 - core)
@@ -66,6 +66,15 @@
 
     ct[0, core] = jnp.transpose(cot[...]).reshape(4, 4, 64, 256)
     sq[core, 0] = jnp.concatenate([row_squares(emb), row_squares(hid), jnp.zeros((6, 256), F32)], axis=0)
+
+    @pl.when(core == 0)
+    def _():
+        nb[0] = emb[...]
+
+    @pl.when(core == 1)
+    def _():
+        nb[1] = hid[...]
+
     pl.semaphore_wait(barrier, 11)
 
     sends = []
@@ -93,24 +102,20 @@
     along_y(1)
     along_y(2)
     n_cp = remote(emb, nb.at[core], sib_s.at[0], sib_r.at[0], sib)
-    l_cp = pltpu.make_async_copy(emb, nb.at[core], loc.at[0])
 
     @pl.when(core == 0)
     def _():
         remote(hid, nb.at[core], sib_s.at[0], sib_r.at[0], sib).start()
-        pltpu.make_async_copy(emb, nb.at[core], loc.at[0]).start()
 
     @pl.when(core == 1)
     def _():
         remote(emb, nb.at[core], sib_s.at[0], sib_r.at[0], sib).start()
-        pltpu.make_async_copy(hid, nb.at[core], loc.at[0]).start()
 
     sends.append(n_cp)
     gain = jnp.where(core == 0, eg[...], hg[...]).reshape(1, PART)
     for cp in sq_cp:
         cp.wait_recv()
     sc[...] = lax.rsqrt((sq[:, 0] + sq[:, 1] + sq[:, 2] + sq[:, 3]) / WIDTH + 1e-6)
-    l_cp.wait()
     n_cp.wait_recv()
     rel_cp[0].wait_recv()
     scale = [jnp.where(core == 0, sc[t, 0:1], sc[t, 1:2]) for t in (0, 1)]
@@ -335,6 +340,11 @@
     def back_spread(ab, d):
         return spread(back_src, midb.at[ab], ab, d, b_s.at[ab, d], b_r.at[ab, d])
 
+    def back_tile(i, d):
+        tx = lax.rem(x + 6 - i, 4)
+        tz = (z + d) % 4
+        return remote(outb.at[tx, tz, :, 1], midb.at[1, z, tx], t_s.at[i, d], t_r.at[i, d], device(x, y, tz, core))
+
     def back_deliver(ab, d, dc):
         return deliver(midb.at[ab], back_dst, ab, d, dc, c_s.at[ab, d, dc], c_r.at[ab, d, dc])
 
@@ -377,7 +387,7 @@
 
     chunks = ((0, 0), (0, 1), (1, 0), (2, 0), (3, 0), (1, 1), (2, 1), (3, 1))
     for turn in range(12):
-        for behind, stage in enumerate((stage_a, stage_b, stage_c, stage_d, stage_e)):
+        for behind, stage in ((0, stage_a), (4, stage_e), (3, stage_d), (2, stage_c), (1, stage_b)):
             if 0 <= turn - behind < 8:
                 stage(*chunks[turn - behind])
         if 1 <= turn <= 3:
@@ -394,10 +404,9 @@
             transpose_root(lt)
             stat_in(0, 0).start()
             stat_in(0, 1).start()
-        if turn == 8:
+        if turn == 9:
             send_owners(0)
-        if turn == 10:
-            pass_owners(0)
+    pass_owners(0)
     send_owners(1)
     pass_owners(1)
     mine = jnp.int32(0)
@@ -425,8 +434,9 @@
             def _():
                 back_spread(0, d).start()
 
-    for d in (2, 1, 3):
-        back_spread(1, d).start()
+        for d in (2, 1, 3):
+            back_tile(i, d).start()
+
     midb[0, x] = outb[x, :, :, 0]
     midb[1, z] = outb[:, z, :, 1]
 
@@ -463,8 +473,9 @@
 
     grams(0, 4)
     for d in (2, 1, 3):
-        for ab in (0, 1):
-            back_spread(ab, d).wait_recv()
+        back_spread(0, d).wait_recv()
+        for i in range(4):
+            back_tile(i, d).wait_recv()
     last = [back_deliver(ab, d, dc) for d, dc in HOPS for ab in (0, 1)]
     for cp in last:
         cp.start()
@@ -474,8 +485,9 @@
     for cp in last:
         cp.wait()
     for d in (2, 1, 3):
-        for ab in (0, 1):
-            back_spread(ab, d).wait_send()
+        back_spread(0, d).wait_send()
+        for i in range(4):
+            back_tile(i, d).wait_send()
 
     for r in range(14):
         update[0, :, r * 1024 : (r + 1) * 1024] = ret[
@@ -523,7 +535,8 @@
             dma((2, 2, 4, 6)), dma((2, 2, 4, 6)), dma((2, 2, 4, 6)), dma((2, 2, 4, 6)),
             dma((2, 4, 2)), dma((2, 4, 2)), dma((4,)),
             dma((2, 2, 4)), dma((2, 2, 4)), dma((2, 2, 4, 2)), dma((2, 2, 4, 2)),
-            dma((2, 4)), dma((2, 4)), dma((2, 4, 2)), dma((2, 4, 2)), dma((2,)), dma((2,)),
+            dma((2, 4)), dma((2, 4)), dma((2, 4, 2)), dma((2, 4, 2)), dma((4, 4)), dma((4, 4)),
+            dma((2,)), dma((2,)),
         ],
         compiler_params=pltpu.CompilerParams(
             collective_id=0, has_side_effects=True, vmem_limit_bytes=62 * 2**20

time: 171 us -> 165 us (0.965)
  Pallas kernels: 161 us -> 155 us
    pallas_call x1, Pallas kernels: 161 us -> 155 us  [step(): pl.pallas_call(reduce_kernel, out_shape=(jax.ShapeDtypeStruct((1024, 1024...]
where the time goes in v5:
time: 165 us; the launch traced here: 164 us
  Pallas kernels  155 us (94%)
  local copies, waits for them, and re-layouts  7.88 us (5%)
    pallas_call x1, Pallas kernels, step(): pl.pallas_call(reduce_kernel, out_shape=(jax.ShapeDtypeStruct((1024, 1024...  155 us
    unnamed x7, local copies, waits for them, and re-layouts  7.88 us

profile of v5, /device:TPU:8, one launch (start us, length us, event | category | flops | bytes accessed | tf_op | source)
XLA Modules:
  0.0 163.7 jit_solution(9482011124593462342)
XLA Ops:
  0.6 155.2 %shampoo.1 = (f32[1024,1024]{1,0:T(8,128)}, f32[1024,1024]{1,0:T(8,128)}, bf16[1,32,14336]{2,1,0:T(8,128)(2,1)}) custom-call(bf16[256,1792]{1,0:T(8,128)(2,1)} %emb.1, bf16[256,1792]{1,0:T(8,128)(2,1)} %hid.1, f32[1792]{0:T(1024)} %eg.1, f32[1792]{0:T(1024)} %hg.1, bf16[256,1024]{1,0:T(8,128)(2,1)} %cot.1, s32[4,14]{1,0:T(4,128)} %own.1, ...), custom_call_target="tpu_custom_call" | custom-call | tf_op jit(solution)/shard_map/shampoo/pallas_call | solution.py:504
  155.8 0.0 copy-start
  155.8 4.9 %copy.16 = f32[1024,1024]{1,0:T(8,128)} copy(f32[1024,1024]{1,0:T(8,128)} %get-tuple-element.6) | data formatting | bytes 8388608
  160.8 0.0 copy-done
  160.8 0.0 copy-start.1
  160.8 2.0 %copy.17 = f32[1024,1024]{1,0:T(8,128)} copy(f32[1024,1024]{1,0:T(8,128)S(1)} %copy-done) | data formatting | bytes 8388608
  162.8 0.0 copy-done.1
  162.8 0.9 copy.18
Async XLA Ops:
  155.8 5.0 %copy-start = (f32[1024,1024]{1,0:T(8,128)S(1)}, f32[1024,1024]{1,0:T(8,128)}, u32[]{:S(2)}) copy-start(f32[1024,1024]{1,0:T(8,128)} %get-tuple-element.7) | copy-start | bytes 12582916
  160.8 2.0 %copy-start.1 = (bf16[1,32,14336]{2,1,0:T(8,128)(2,1)S(1)}, bf16[1,32,14336]{2,1,0:T(8,128)(2,1)}, u32[]{:S(2)}) copy-start(bf16[1,32,14336]{2,1,0:T(8,128)(2,1)} %get-tuple-element.8) | copy-start | bytes 2752516

commit v6 on v5

--- a/solution.py
+++ b/solution.py
@@ -41,7 +41,7 @@
 
 def reduce_kernel(
     emb, hid, eg, hg, cot, own, lstat, rstat, lroot, rroot, lnew, rnew, update,
-    ct, nb, sq, sc, part, r1, r2, yb, sh, blocks, outb, arr, ret, tb, rt, lt, st, so, mid, midb,
+    ct, nb, sq, sc, part, r1, r2, yb, sh, blocks, outb, arr, ret, tb, rt, lt, st, so, mid, midb, rows_sm,
     sq_s, sq_r, sib_s, sib_r, ct_s, ct_r, rel_s, rel_r, p1_s, p1_r, p2_s, p2_r, y_s, y_r, loc,
     o_s, o_r, q_s, q_r, b_s, b_r, c_s, c_r, t_s, t_r, st_i, st_o,
 ):
@@ -366,9 +366,9 @@
                 blocks[u, r, :, done : done + size] = sh[u, i, :, lane : lane + size]
                 done += size
 
-        @pl.loop(0, 32)
+        @pl.loop(0, 32, unroll=8)
         def _(t):
-            outb[t // 8, (t // 2) % 4, t % 2, u] = blocks[u, row_of(t)]
+            outb[t // 8, (t // 2) % 4, t % 2, u] = blocks[u, rows_sm[t]]
 
         passing[1, u] = owner_spread(u)
         for cp in passing[1, u]:
@@ -399,6 +399,12 @@
             transpose_root(rt)
             l_root = pltpu.make_async_copy(lroot, tb, loc.at[3])
             l_root.start()
+        if turn == 6:
+
+            @pl.loop(0, 32)
+            def _(t):
+                rows_sm[t] = row_of(t)
+
         if turn == 5:
             l_root.wait()
             transpose_root(lt)
@@ -531,6 +537,7 @@
             pltpu.VMEM((2, 128, 1024), F32),
             pltpu.VMEM((2, 2, 4, 4, 2, 16, 512), BF16),
             pltpu.VMEM((2, 4, 4, 2, 16, 1024), BF16),
+            pltpu.SMEM((32,), jnp.int32),
             dma((2, 4)), dma((2, 4)), dma((1,)), dma((1,)), dma((3,)), dma((3,)), dma((4,)), dma((4,)),
             dma((2, 2, 4, 6)), dma((2, 2, 4, 6)), dma((2, 2, 4, 6)), dma((2, 2, 4, 6)),
             dma((2, 4, 2)), dma((2, 4, 2)), dma((4,)),

time: 165 us -> 164 us (level)
  no operation moved by 1% of the time
where the time goes in v6:
time: 164 us; the launch traced here: 163 us
  Pallas kernels  155 us (95%)
  local copies, waits for them, and re-layouts  7.88 us (5%)
    pallas_call x1, Pallas kernels, step(): pl.pallas_call(reduce_kernel, out_shape=(jax.ShapeDtypeStruct((1024, 1024...  155 us
    unnamed x7, local copies, waits for them, and re-layouts  7.88 us

profile of v6, /device:TPU:8, one launch (start us, length us, event | category | flops | bytes accessed | tf_op | source)
XLA Modules:
  0.0 163.4 jit_solution(12299872130271327017)
XLA Ops:
  0.6 154.9 %shampoo.1 = (f32[1024,1024]{1,0:T(8,128)}, f32[1024,1024]{1,0:T(8,128)}, bf16[1,32,14336]{2,1,0:T(8,128)(2,1)}) custom-call(bf16[256,1792]{1,0:T(8,128)(2,1)} %emb.1, bf16[256,1792]{1,0:T(8,128)(2,1)} %hid.1, f32[1792]{0:T(1024)} %eg.1, f32[1792]{0:T(1024)} %hg.1, bf16[256,1024]{1,0:T(8,128)(2,1)} %cot.1, s32[4,14]{1,0:T(4,128)} %own.1, ...), custom_call_target="tpu_custom_call" | custom-call | tf_op jit(solution)/shard_map/shampoo/pallas_call | solution.py:510
  155.5 0.0 copy-start
  155.5 4.9 %copy.16 = f32[1024,1024]{1,0:T(8,128)} copy(f32[1024,1024]{1,0:T(8,128)} %get-tuple-element.6) | data formatting | bytes 8388608
  160.5 0.0 copy-done
  160.5 0.0 copy-start.1
  160.5 2.0 %copy.17 = f32[1024,1024]{1,0:T(8,128)} copy(f32[1024,1024]{1,0:T(8,128)S(1)} %copy-done) | data formatting | bytes 8388608
  162.5 0.0 copy-done.1
  162.5 0.9 copy.18
Async XLA Ops:
  155.5 5.0 %copy-start = (f32[1024,1024]{1,0:T(8,128)S(1)}, f32[1024,1024]{1,0:T(8,128)}, u32[]{:S(2)}) copy-start(f32[1024,1024]{1,0:T(8,128)} %get-tuple-element.7) | copy-start | bytes 12582916
  160.5 2.0 %copy-start.1 = (bf16[1,32,14336]{2,1,0:T(8,128)(2,1)S(1)}, bf16[1,32,14336]{2,1,0:T(8,128)(2,1)}, u32[]{:S(2)}) copy-start(bf16[1,32,14336]{2,1,0:T(8,128)(2,1)} %get-tuple-element.8) | copy-start | bytes 2752516
